TPU v7x, 32 devices: a whole 2x2x4 slice. The times are simulated.
32 devices in a mesh: sec: 4 (over x, core), tile: 8 (over z, y).
Axes of the slice: x: 2, y: 2, z: 4, core: 2. Of those that a mesh axis runs over, the one named last changes fastest.
Arguments:
- velocity: float32 [3, 96, 16, 128], P(None, 'sec', 'tile'), may hold values from -5 to 8
- prev_tendency: float32 [3, 96, 16, 128], P(None, 'sec', 'tile'), may hold values from -12 to 12
- disk_cells: int32 [4, 8, 256], P('sec', 'tile'), may hold values from 0 to 6144, as said below
- disk_kind: int32 [4, 8, 256], P('sec', 'tile'), may hold values from 0 to 15
- rotor_weights: float32 [16], replicated, may hold values from 0.5 to 2
Outputs:
- velocity_next: float32 [3, 96, 16, 128], P(None, 'sec', 'tile')
- tendency: float32 [3, 96, 16, 128], P(None, 'sec', 'tile')
Inputs may be any that keep to these rules, and one draw needn't show every extreme that they name: `disk_cells`: an entry equal to 6144 marks an empty slot; any other entry is a flat index (i * 2 + j) * 128 + k into the device's own block, repeats allowed. Every slot of a device in the first half of the sec indices is empty; some other device has all 256 slots live in every draw.
All inputs are finite; a program needn't handle non-finite values.
Results may differ from a plain program's by a relative error of at most 0.0003.
Values sent between devices are 32-bit elements; how exact they have to be, the bound alone decides.
A program may use at most 64 MiB of HBM per device.

v0:
```python
import math

import jax
import jax.numpy as jnp
from jax import lax
from jax.sharding import PartitionSpec as P

STEPS = 2
KINDS = 16


precise = lax.Precision.HIGHEST
time_step = 0.1
fringe_rate = 2.0
smag_coef = 0.04


def extended_2(block, sides, width):
    for axis, dim in sides:
        count = lax.axis_size(axis)
        forward = [(i, i + 1) for i in range(count - 1)]
        forward.append((count - 1, 0))
        backward = [(target, source) for source, target in forward]
        low = lax.ppermute(
            lax.slice_in_dim(block, block.shape[dim] - width, None, axis=dim), axis, forward
        )
        high = lax.ppermute(lax.slice_in_dim(block, 0, width, axis=dim), axis, backward)
        block = jnp.concatenate([low, block, high], axis=dim)
    return block


def from_root(block, axis, owner):
    block = jnp.where(lax.axis_index(axis) == owner, block, jnp.zeros_like(block))
    return lax.psum(block, axis)


def gradients(padded, z_sign):
    centre = padded[:, 1:-1, 1:-1, :]
    grad_x = 0.5 * (padded[:, 2:, 1:-1, :] - padded[:, :-2, 1:-1, :])
    grad_y = 0.5 * (padded[:, 1:-1, 2:, :] - padded[:, 1:-1, :-2, :])
    extended = jnp.concatenate(
        [z_sign * centre[..., :1], centre, z_sign * centre[..., -1:]], axis=-1
    )
    grad_z = 0.5 * (extended[..., 2:] - extended[..., :-2])
    return (grad_x, grad_y, grad_z)


def strain_stress(slopes):

    def strain(first, second):
        return 0.5 * (slopes[second][first] + slopes[first][second])

    strain_xx = strain(0, 0)
    strain_yy = strain(1, 1)
    strain_zz = strain(2, 2)
    strain_xy = strain(0, 1)
    strain_xz = strain(0, 2)
    strain_yz = strain(1, 2)
    squared = strain_xx * strain_xx + strain_yy * strain_yy + strain_zz * strain_zz
    squared = squared + 2.0 * (
        strain_xy * strain_xy + strain_xz * strain_xz + strain_yz * strain_yz
    )
    double = 2.0 * (smag_coef * jnp.sqrt(2.0 * squared + 0.01))
    return jnp.stack(
        [
            double * strain_xx,
            double * strain_yy,
            double * strain_zz,
            double * strain_xy,
            double * strain_xz,
            double * strain_yz,
        ]
    )


def advection(slopes, centre):
    return centre[0:1] * slopes[0] + centre[1:2] * slopes[1] + centre[2:3] * slopes[2]


def stress_force(padded):
    grad_x, grad_y, grad_z = gradients(padded, 0.0)
    return jnp.stack(
        [
            grad_x[0] + grad_y[3] + grad_z[4],
            grad_x[3] + grad_y[1] + grad_z[5],
            grad_x[4] + grad_y[5] + grad_z[2],
        ]
    )


def faces(source):
    return extended_2(source, (("sec", 1), ("tile", 2)), 1)


def sec_turn(blocks):
    return lax.all_to_all(blocks, "sec", split_axis=0, concat_axis=0, tiled=True)


def tile_turn(blocks):
    return lax.all_to_all(blocks, "tile", split_axis=0, concat_axis=0, tiled=True)


def hartley_table(length):
    index_row = jnp.arange(length)
    product = index_row[:, None] * index_row[None, :] % length
    angle = 2.0 * math.pi / length * product.astype(jnp.float32)
    return jnp.cos(angle) + jnp.sin(angle)


def local(velocity, prev_tendency, disk_cells, disk_kind, rotor_weights):
    sec_count = lax.axis_size("sec")
    tile_count = lax.axis_size("tile")
    sec_at = lax.axis_index("sec")
    tile_at = lax.axis_index("tile")
    slab_x = velocity.shape[1]
    tile_y = velocity.shape[2]
    depth_z = velocity.shape[3]
    full_x = slab_x * sec_count
    full_y = tile_y * tile_count
    part_z = depth_z // sec_count
    modes_each = slab_x * depth_z // tile_count
    cell_count = slab_x * tile_y * depth_z
    modes = jnp.arange(depth_z).astype(jnp.float32)[:, None]
    points = jnp.arange(depth_z).astype(jnp.float32)[None, :] + 0.5
    cos_blocks = jnp.cos(math.pi * modes * points / depth_z).reshape(sec_count, part_z, depth_z)
    weight_blocks = jnp.where(jnp.arange(depth_z) == 0, 1.0 / depth_z, 2.0 / depth_z).astype(
        jnp.float32
    )
    weight_blocks = weight_blocks.reshape(sec_count, part_z)
    x_table = hartley_table(full_x)
    y_table = hartley_table(full_y).reshape(full_y, tile_count, tile_y)
    flat_ids = tile_at * modes_each + jnp.arange(modes_each)
    mode_x = flat_ids // part_z
    mode_z = sec_at * part_z + flat_ids % part_z
    mode_y = jnp.arange(full_y)
    sin_x = jnp.sin(2.0 * math.pi * mode_x.astype(jnp.float32) / full_x)
    sin_y = jnp.sin(2.0 * math.pi * mode_y.astype(jnp.float32) / full_y)
    sin_z = jnp.sin(math.pi * mode_z.astype(jnp.float32) / depth_z)
    eigen = -((sin_x * sin_x)[:, None] + (sin_y * sin_y)[None, :] + (sin_z * sin_z)[:, None])
    zero_mode = (
        (mode_x % (full_x // 2) == 0)[:, None]
        & (mode_y % (full_y // 2) == 0)[None, :]
        & (mode_z == 0)[:, None]
    )
    recip = jnp.where(zero_mode, 0.0, 1.0 / jnp.where(zero_mode, 1.0, eigen))
    slab_pos = jnp.sin(math.pi * (jnp.arange(slab_x).astype(jnp.float32) + 0.5) / slab_x)
    lam_x = fringe_rate * (slab_pos * slab_pos)
    flag = (
        (sec_at == 0)
        | (sec_at == sec_count // 2)
        | (sec_at == 3 * sec_count // 4)
        | (sec_at == sec_count - 1)
    ).astype(jnp.float32)
    picked = disk_cells.reshape(-1)
    kinds = disk_kind.reshape(-1)
    live = picked < cell_count
    safe = jnp.minimum(picked, cell_count - 1)
    weight = jnp.sum(
        jnp.where(kinds[:, None] == jnp.arange(KINDS)[None, :], rotor_weights[None, :], 0.0), axis=1
    )
    current = velocity
    tendency_old = prev_tendency
    tendency = prev_tendency
    for step_no in range(STEPS):
        wide = extended_2(current, (("sec", 1), ("tile", 2)), 2)
        wide_slopes = gradients(wide, -1.0)
        push_field = stress_force(strain_stress(wide_slopes))
        slopes = tuple((piece[:, 1:-1, 1:-1, :] for piece in wide_slopes))
        advect = advection(slopes, current)
        target = from_root(current, "sec", sec_count // 2 - 1)
        fringe = flag * lam_x[None, :, None, None] * (target - current)
        sampled = current[0].reshape(-1)[safe]
        push = jnp.where(live, -(weight * sampled * jnp.abs(sampled)), 0.0)
        turbine = (
            jnp.zeros((cell_count,), jnp.float32)
            .at[safe]
            .add(push)
            .reshape(slab_x, tile_y, depth_z)
        )
        empty = jnp.zeros_like(turbine)
        tendency = push_field - advect + jnp.stack([turbine, empty, empty]) + fringe
        interim = current + time_step * (1.5 * tendency - 0.5 * tendency_old)
        grad_x, grad_y, grad_z = gradients(faces(interim), -1.0)
        rhs = grad_x[0] + grad_y[1] + grad_z[2]
        coeffs = jnp.einsum("xyz,bcz->bxyc", rhs, cos_blocks, precision=precise)
        gathered = sec_turn(coeffs).reshape(full_x, tile_y, part_z)
        along_x = jnp.einsum("xyc,kx->kcy", gathered, x_table, precision=precise)
        spread = tile_turn(along_x.reshape(tile_count, modes_each, tile_y))
        along_y = jnp.einsum("sqt,lst->ql", spread, y_table, precision=precise)
        scaled = along_y * recip
        back_y = jnp.einsum("ql,lst->sqt", scaled, y_table, precision=precise) / (full_x * full_y)
        returned = tile_turn(back_y).reshape(full_x, part_z, tile_y)
        back_x = jnp.einsum("kcy,kx->xyc", returned, x_table, precision=precise)
        home = sec_turn(back_x.reshape(sec_count, slab_x, tile_y, part_z))
        pressure = jnp.einsum(
            "bxyc,bcz->xyz", home * weight_blocks[:, None, None, :], cos_blocks, precision=precise
        )
        press_x, press_y, press_z = gradients(faces(pressure[None]), 1.0)
        current = interim - jnp.concatenate([press_x, press_y, press_z], axis=0)
        tendency_old = tendency
    return (current, tendency)


def solution(mesh):
    in_specs = (
        P(None, "sec", "tile", None),
        P(None, "sec", "tile", None),
        P("sec", "tile", None),
        P("sec", "tile", None),
        P(),
    )
    out_specs = (P(None, "sec", "tile", None), P(None, "sec", "tile", None))
    return jax.shard_map(local, mesh=mesh, in_specs=in_specs, out_specs=out_specs, check_vma=False)
```

profile of v0, /device:TPU:0, one launch (start us, length us, event | category | flops | bytes accessed | tf_op | source)
XLA Modules:
  0.0 218.1 jit_solution(1880339886588055885)
XLA Ops:
  9.3 2.0 collective-permute-start.1
  12.1 1.7 gather_fusion
  14.7 2.4 %scatter_custom_fusion = f32[6144]{0:T(1024)S(1)} fusion(s32[256]{0:T(256)S(1)} %bitcast.147, f32[256]{0:T(256)S(1)} %negate_select_fusion.6, f32[]{:T(128)} %constant.144.clone.1), kind=kCustom, calls=%fused_computation.290 | custom fusion | flops 256 | bytes 24580 | tf_op jit(solution)/shard_map/scatter-add | solution.py:177
  17.1 2.3 %collective-permute-start.2 = (f32[3,28,2,128]{3,1,2,0:T(8,128)S(1)}, f32[3,28,2,128]{3,1,2,0:T(8,128)S(1)}, u32[]{:S(2)}, u32[]{:S(2)}) collective-permute-start(f32[3,28,2,128]{3,1,2,0:T(8,128)S(1)} %pad_maximum_fusion.22), channel_id=1, source_target_pairs={{0,1},{1,2},{2,3},{3,4},{4,5},{5,6},{6,7},{7,0},{8,9},{9,10},{10,1... | collective-permute-start | bytes 258056 | tf_op jit(solution)/shard_map/ppermute | solution.py:24
  19.5 3.1 %collective-permute-start.3 = (f32[3,28,2,128]{3,1,2,0:T(8,128)S(1)}, f32[3,28,2,128]{3,1,2,0:T(8,128)S(1)}, u32[]{:S(2)}, u32[]{:S(2)}) collective-permute-start(f32[3,28,2,128]{3,1,2,0:T(8,128)S(1)} %pad_maximum_fusion.22), channel_id=1, source_target_pairs={{1,0},{2,1},{3,2},{4,3},{5,4},{6,5},{7,6},{0,7},{9,8},{10,9},{11,1... | collective-permute-start | bytes 258056 | tf_op jit(solution)/shard_map/ppermute | solution.py:27
  22.6 2.8 %collective-permute-done.2 = f32[3,28,2,128]{3,1,2,0:T(8,128)S(1)} collective-permute-done((f32[3,28,2,128]{3,1,2,0:T(8,128)S(1)}, f32[3,28,2,128]{3,1,2,0:T(8,128)S(1)}, u32[]{:S(2)}, u32[]{:S(2)}) %collective-permute-start.2) | collective-permute-done | bytes 86048 | tf_op jit(solution)/shard_map/ppermute | solution.py:24
  27.2 15.7 %all-reduce.5.cloned.1.call-done = f32[3,24,2,128]{3,1,2,0:T(8,128)} async-done(((f32[3,24,2,128]{3,1,2,0:T(8,128)}), f32[3,24,2,128]{3,1,2,0:T(8,128)}) %all-reduce.5.cloned.1.call-update) | async-done | bytes 73744 | tf_op jit(solution)/shard_map/psum | solution.py:34
  48.1 4.3 %collective-permute-start.6 = (f32[3,26,1,128]{3,1,2,0:T(8,128)S(1)}, f32[3,26,1,128]{3,1,2,0:T(8,128)S(1)}, u32[]{:S(2)}, u32[]{:S(2)}) collective-permute-start(f32[3,26,1,128]{3,1,2,0:T(8,128)S(1)} %get-tuple-element.47), channel_id=1, source_target_pairs={{1,0},{2,1},{3,2},{4,3},{5,4},{6,5},{7,6},{0,7},{9,8},{10,9},{11,1... | collective-permute-start | bytes 119816 | tf_op jit(solution)/shard_map/ppermute | solution.py:27
  54.2 5.0 %collective-permute-done.7 = f32[3,26,1,128]{3,1,2,0:T(8,128)S(1)} collective-permute-done((f32[3,26,1,128]{3,1,2,0:T(8,128)S(1)}, f32[3,26,1,128]{3,1,2,0:T(8,128)S(1)}, u32[]{:S(2)}, u32[]{:S(2)}) %collective-permute-start.7) | collective-permute-done | bytes 39968 | tf_op jit(solution)/shard_map/ppermute | solution.py:24
  60.6 3.3 %all-to-all-start = ((f32[4,1,1536]{2,1,0:T(1,128)}), f32[4,1,1536]{2,1,0:T(1,128)S(1)}, u32[]{:S(2)}, u32[]{:S(2)}) async-start(f32[4,1,1536]{2,1,0:T(1,128)} %reshape.249), calls=%async_computation | async-start | bytes 49152 | tf_op jit(solution)/shard_map/all_to_all | solution.py:96
  63.9 3.9 %all-to-all-done = f32[4,1,1536]{2,1,0:T(1,128)S(1)} async-done(((f32[4,1,1536]{2,1,0:T(1,128)}), f32[4,1,1536]{2,1,0:T(1,128)S(1)}, u32[]{:S(2)}, u32[]{:S(2)}) %all-to-all-start) | async-done | bytes 24608 | tf_op jit(solution)/shard_map/all_to_all | solution.py:96
  70.5 3.3 %all-to-all-start.1 = ((f32[8,384,2]{1,2,0:T(2,128)}), f32[8,384,2]{1,2,0:T(2,128)S(1)}, u32[]{:S(2)}, u32[]{:S(2)}) async-start(f32[8,384,2]{1,2,0:T(2,128)} %copy.93), calls=%async_computation.1 | async-start | bytes 49152 | tf_op jit(solution)/shard_map/all_to_all | solution.py:100
  73.9 6.5 %all-to-all-done.1 = f32[8,384,2]{1,2,0:T(2,128)S(1)} async-done(((f32[8,384,2]{1,2,0:T(2,128)}), f32[8,384,2]{1,2,0:T(2,128)S(1)}, u32[]{:S(2)}, u32[]{:S(2)}) %all-to-all-start.1) | async-done | bytes 24608 | tf_op jit(solution)/shard_map/all_to_all | solution.py:100
  81.1 9.0 %all_to_all.40 = f32[8,384,2]{1,2,0:T(2,128)S(1)} all-to-all(f32[8,384,2]{1,2,0:T(2,128)S(1)} %copy.95), channel_id=1, replica_groups=mesh['sec'=4,'tile'=8] {'tile'}, dimensions={0} | all-to-all | bytes 49152 | tf_op jit(solution)/shard_map/all_to_all | solution.py:100
  91.6 3.3 %all-to-all-start.3 = ((f32[4,1,1536]{2,1,0:T(1,128)}), f32[4,1,1536]{2,1,0:T(1,128)S(1)}, u32[]{:S(2)}, u32[]{:S(2)}) async-start(f32[4,1,1536]{2,1,0:T(1,128)} %reshape.251), calls=%async_computation.3 | async-start | bytes 49152 | tf_op jit(solution)/shard_map/all_to_all | solution.py:96
  94.9 3.8 %all-to-all-done.3 = f32[4,1,1536]{2,1,0:T(1,128)S(1)} async-done(((f32[4,1,1536]{2,1,0:T(1,128)}), f32[4,1,1536]{2,1,0:T(1,128)S(1)}, u32[]{:S(2)}, u32[]{:S(2)}) %all-to-all-start.3) | async-done | bytes 24608 | tf_op jit(solution)/shard_map/all_to_all | solution.py:96
  101.4 1.8 collective-permute-done.9
  107.0 3.3 %collective-permute-done.11 = f32[1,26,1,128]{3,1,2,0:T(8,128)S(1)} collective-permute-done((f32[1,26,1,128]{3,1,2,0:T(8,128)S(1)}, f32[1,26,1,128]{3,1,2,0:T(8,128)S(1)}, u32[]{:S(2)}, u32[]{:S(2)}) %collective-permute-start.11) | collective-permute-done | bytes 13344 | tf_op jit(solution)/shard_map/ppermute | solution.py:24
  111.1 1.7 collective-permute-start.13
  112.8 1.7 gather_fusion.1
  114.7 4.7 %collective-permute-start.15 = (f32[3,28,2,128]{3,1,2,0:T(8,128)S(1)}, f32[3,28,2,128]{3,1,2,0:T(8,128)S(1)}, u32[]{:S(2)}, u32[]{:S(2)}) collective-permute-start(f32[3,28,2,128]{3,1,2,0:T(8,128)S(1)} %pad_maximum_fusion.24), channel_id=1, source_target_pairs={{1,0},{2,1},{3,2},{4,3},{5,4},{6,5},{7,6},{0,7},{9,8},{10,9},{11,1... | collective-permute-start | bytes 258056 | tf_op jit(solution)/shard_map/ppermute | solution.py:27
  119.4 2.3 %scatter_custom_fusion.1 = f32[6144]{0:T(1024)S(1)} fusion(s32[256]{0:T(256)S(1)} %bitcast.148, f32[256]{0:T(256)S(1)} %negate_select_fusion.5, f32[]{:T(128)} %constant.144.clone.1), kind=kCustom, calls=%fused_computation.288 | custom fusion | flops 256 | bytes 24580 | tf_op jit(solution)/shard_map/scatter-add | solution.py:177
  124.1 23.8 %all-reduce.7.cloned.1.call-done = f32[3,24,2,128]{3,1,2,0:T(8,128)} async-done(((f32[3,24,2,128]{3,1,2,0:T(8,128)}), f32[3,24,2,128]{3,1,2,0:T(8,128)}) %all-reduce.7.cloned.1.call-update) | async-done | bytes 73744 | tf_op jit(solution)/shard_map/psum | solution.py:34
  151.4 1.7 collective-permute-done.17
  153.1 4.3 %collective-permute-start.18 = (f32[3,26,1,128]{3,1,2,0:T(8,128)S(1)}, f32[3,26,1,128]{3,1,2,0:T(8,128)S(1)}, u32[]{:S(2)}, u32[]{:S(2)}) collective-permute-start(f32[3,26,1,128]{3,1,2,0:T(8,128)S(1)} %get-tuple-element.45), channel_id=1, source_target_pairs={{1,0},{2,1},{3,2},{4,3},{5,4},{6,5},{7,6},{0,7},{9,8},{10,9},{11,1... | collective-permute-start | bytes 119816 | tf_op jit(solution)/shard_map/ppermute | solution.py:27
  159.2 5.0 %collective-permute-done.19 = f32[3,26,1,128]{3,1,2,0:T(8,128)S(1)} collective-permute-done((f32[3,26,1,128]{3,1,2,0:T(8,128)S(1)}, f32[3,26,1,128]{3,1,2,0:T(8,128)S(1)}, u32[]{:S(2)}, u32[]{:S(2)}) %collective-permute-start.19) | collective-permute-done | bytes 39968 | tf_op jit(solution)/shard_map/ppermute | solution.py:24
  165.0 6.4 %all_to_all.41 = f32[4,1,1536]{2,1,0:T(1,128)S(1)} all-to-all(f32[4,1,1536]{2,1,0:T(1,128)S(1)} %reshape.253), channel_id=1, replica_groups=mesh['sec'=4,'tile'=8] {'sec'}, dimensions={0} | all-to-all | bytes 49152 | tf_op jit(solution)/shard_map/all_to_all | solution.py:96
  173.1 9.0 %all_to_all.42 = f32[8,384,2]{1,2,0:T(2,128)S(1)} all-to-all(f32[8,384,2]{1,2,0:T(2,128)S(1)} %copy.103), channel_id=1, replica_groups=mesh['sec'=4,'tile'=8] {'tile'}, dimensions={0} | all-to-all | bytes 49152 | tf_op jit(solution)/shard_map/all_to_all | solution.py:100
  182.8 9.0 %all_to_all.43 = f32[8,384,2]{1,2,0:T(2,128)S(1)} all-to-all(f32[8,384,2]{1,2,0:T(2,128)S(1)} %copy.105), channel_id=1, replica_groups=mesh['sec'=4,'tile'=8] {'tile'}, dimensions={0} | all-to-all | bytes 49152 | tf_op jit(solution)/shard_map/all_to_all | solution.py:100
  192.6 6.3 %all_to_all.44 = f32[4,1,1536]{2,1,0:T(1,128)S(1)} all-to-all(f32[4,1,1536]{2,1,0:T(1,128)S(1)} %reshape.255), channel_id=1, replica_groups=mesh['sec'=4,'tile'=8] {'sec'}, dimensions={0} | all-to-all | bytes 49152 | tf_op jit(solution)/shard_map/all_to_all | solution.py:96
  201.6 1.8 collective-permute-done.21
  207.2 3.3 %collective-permute-done.23 = f32[1,26,1,128]{3,1,2,0:T(8,128)S(1)} collective-permute-done((f32[1,26,1,128]{3,1,2,0:T(8,128)S(1)}, f32[1,26,1,128]{3,1,2,0:T(8,128)S(1)}, u32[]{:S(2)}, u32[]{:S(2)}) %collective-permute-start.23) | collective-permute-done | bytes 13344 | tf_op jit(solution)/shard_map/ppermute | solution.py:24
  (175 shorter events, 44.6 us)
Async XLA Ops:
  7.2 35.8 %all-reduce.5.cloned.1.call-start = ((), (), s32[]{:S(2)}) async-start(), calls=%async_computation.8 | async-start | bytes 147456 | tf_op jit(solution)/shard_map/psum | solution.py:34
  8.7 2.5 %copy-start = (f32[3,24,2,128]{3,2,1,0:T(2,128)S(1)}, f32[3,24,2,128]{3,2,1,0:T(2,128)}, u32[]{:S(2)}) copy-start(f32[3,24,2,128]{3,2,1,0:T(2,128)} %param.5) | copy-start | bytes 221188
  8.8 8.3 %collective-permute-start = (f32[3,2,2,128]{3,1,2,0:T(2,128)S(1)}, f32[3,2,2,128]{3,1,2,0:T(2,128)S(1)}, u32[]{:S(2)}, u32[]{:S(2)}) collective-permute-start(f32[3,2,2,128]{3,1,2,0:T(2,128)S(1)} %get-tuple-element.66), channel_id=1, source_target_pairs={{0,8},{8,16},{16,24},{24,0},{1,9},{9,17},{17,25},{25,1},{2,10},{10... | collective-permute-start | bytes 18440 | tf_op jit(solution)/shard_map/ppermute | solution.py:24
  9.3 7.9 %collective-permute-start.1 = (f32[3,2,2,128]{3,1,2,0:T(2,128)S(1)}, f32[3,2,2,128]{3,1,2,0:T(2,128)S(1)}, u32[]{:S(2)}, u32[]{:S(2)}) collective-permute-start(f32[3,2,2,128]{3,1,2,0:T(2,128)S(1)} %get-tuple-element.67), channel_id=1, source_target_pairs={{8,0},{16,8},{24,16},{0,24},{9,1},{17,9},{25,17},{1,25},{10,2},{18... | collective-permute-start | bytes 18440 | tf_op jit(solution)/shard_map/ppermute | solution.py:27
  11.3 0.7 copy-start.2
  17.1 8.3 %collective-permute-start.2 = (f32[3,28,2,128]{3,1,2,0:T(8,128)S(1)}, f32[3,28,2,128]{3,1,2,0:T(8,128)S(1)}, u32[]{:S(2)}, u32[]{:S(2)}) collective-permute-start(f32[3,28,2,128]{3,1,2,0:T(8,128)S(1)} %pad_maximum_fusion.22), channel_id=1, source_target_pairs={{0,1},{1,2},{2,3},{3,4},{4,5},{5,6},{6,7},{7,0},{8,9},{9,10},{10,1... | collective-permute-start | bytes 258056 | tf_op jit(solution)/shard_map/ppermute | solution.py:24
  19.5 6.7 %collective-permute-start.3 = (f32[3,28,2,128]{3,1,2,0:T(8,128)S(1)}, f32[3,28,2,128]{3,1,2,0:T(8,128)S(1)}, u32[]{:S(2)}, u32[]{:S(2)}) collective-permute-start(f32[3,28,2,128]{3,1,2,0:T(8,128)S(1)} %pad_maximum_fusion.22), channel_id=1, source_target_pairs={{1,0},{2,1},{3,2},{4,3},{5,4},{6,5},{7,6},{0,7},{9,8},{10,9},{11,1... | collective-permute-start | bytes 258056 | tf_op jit(solution)/shard_map/ppermute | solution.py:27
  27.2 15.8 %copy-start.1 = (f32[3,24,2,128]{3,2,1,0:T(2,128)S(1)}, f32[3,24,2,128]{3,2,1,0:T(2,128)}, u32[]{:S(2)}) copy-start(f32[3,24,2,128]{3,2,1,0:T(2,128)} %param.6) | copy-start | bytes 221188
  44.0 2.4 %collective-permute-start.4 = (f32[3,1,2,128]{3,1,2,0:T(1,128)S(1)}, f32[3,1,2,128]{3,1,2,0:T(1,128)S(1)}, u32[]{:S(2)}, u32[]{:S(2)}) collective-permute-start(f32[3,1,2,128]{3,1,2,0:T(1,128)S(1)} %get-tuple-element.59), channel_id=1, source_target_pairs={{8,0},{16,8},{24,16},{0,24},{9,1},{17,9},{25,17},{1,25},{10,2},{18... | collective-permute-start | bytes 9224 | tf_op jit(solution)/shard_map/ppermute | solution.py:27
  45.1 3.0 %collective-permute-start.5 = (f32[3,1,2,128]{3,1,2,0:T(1,128)S(1)}, f32[3,1,2,128]{3,1,2,0:T(1,128)S(1)}, u32[]{:S(2)}, u32[]{:S(2)}) collective-permute-start(f32[3,1,2,128]{3,1,2,0:T(1,128)S(1)} %get-tuple-element.58), channel_id=1, source_target_pairs={{0,8},{8,16},{16,24},{24,0},{1,9},{9,17},{17,25},{25,1},{2,10},{10... | collective-permute-start | bytes 9224 | tf_op jit(solution)/shard_map/ppermute | solution.py:24
  48.1 6.0 %collective-permute-start.6 = (f32[3,26,1,128]{3,1,2,0:T(8,128)S(1)}, f32[3,26,1,128]{3,1,2,0:T(8,128)S(1)}, u32[]{:S(2)}, u32[]{:S(2)}) collective-permute-start(f32[3,26,1,128]{3,1,2,0:T(8,128)S(1)} %get-tuple-element.47), channel_id=1, source_target_pairs={{1,0},{2,1},{3,2},{4,3},{5,4},{6,5},{7,6},{0,7},{9,8},{10,9},{11,1... | collective-permute-start | bytes 119816 | tf_op jit(solution)/shard_map/ppermute | solution.py:27
  52.4 6.8 %collective-permute-start.7 = (f32[3,26,1,128]{3,1,2,0:T(8,128)S(1)}, f32[3,26,1,128]{3,1,2,0:T(8,128)S(1)}, u32[]{:S(2)}, u32[]{:S(2)}) collective-permute-start(f32[3,26,1,128]{3,1,2,0:T(8,128)S(1)} %get-tuple-element.46), channel_id=1, source_target_pairs={{0,1},{1,2},{2,3},{3,4},{4,5},{5,6},{6,7},{7,0},{8,9},{9,10},{10,1... | collective-permute-start | bytes 119816 | tf_op jit(solution)/shard_map/ppermute | solution.py:24
  60.6 7.1 %all-to-all-start = ((f32[4,1,1536]{2,1,0:T(1,128)}), f32[4,1,1536]{2,1,0:T(1,128)S(1)}, u32[]{:S(2)}, u32[]{:S(2)}) async-start(f32[4,1,1536]{2,1,0:T(1,128)} %reshape.249), calls=%async_computation | async-start | bytes 49152 | tf_op jit(solution)/shard_map/all_to_all | solution.py:96
  70.5 9.9 %all-to-all-start.1 = ((f32[8,384,2]{1,2,0:T(2,128)}), f32[8,384,2]{1,2,0:T(2,128)S(1)}, u32[]{:S(2)}, u32[]{:S(2)}) async-start(f32[8,384,2]{1,2,0:T(2,128)} %copy.93), calls=%async_computation.1 | async-start | bytes 49152 | tf_op jit(solution)/shard_map/all_to_all | solution.py:100
  91.6 7.1 %all-to-all-start.3 = ((f32[4,1,1536]{2,1,0:T(1,128)}), f32[4,1,1536]{2,1,0:T(1,128)S(1)}, u32[]{:S(2)}, u32[]{:S(2)}) async-start(f32[4,1,1536]{2,1,0:T(1,128)} %reshape.251), calls=%async_computation.3 | async-start | bytes 49152 | tf_op jit(solution)/shard_map/all_to_all | solution.py:96
  94.8 53.1 %all-reduce.7.cloned.1.call-start = ((), (), s32[]{:S(2)}) async-start(), calls=%async_computation.9 | async-start | bytes 147456 | tf_op jit(solution)/shard_map/psum | solution.py:34
  100.0 1.4 collective-permute-start.8
  100.1 3.0 %collective-permute-start.9 = (f32[1,1,2,128]{3,1,2,0:T(1,128)S(1)}, f32[1,1,2,128]{3,1,2,0:T(1,128)S(1)}, u32[]{:S(2)}, u32[]{:S(2)}) collective-permute-start(f32[1,1,2,128]{3,1,2,0:T(1,128)S(1)} %get-tuple-element.84), channel_id=1, source_target_pairs={{0,8},{8,16},{16,24},{24,0},{1,9},{9,17},{17,25},{25,1},{2,10},{10... | collective-permute-start | bytes 3080 | tf_op jit(solution)/shard_map/ppermute | solution.py:24
  103.2 3.8 %collective-permute-start.10 = (f32[1,26,1,128]{3,1,2,0:T(8,128)S(1)}, f32[1,26,1,128]{3,1,2,0:T(8,128)S(1)}, u32[]{:S(2)}, u32[]{:S(2)}) collective-permute-start(f32[1,26,1,128]{3,1,2,0:T(8,128)S(1)} %get-tuple-element.72), channel_id=1, source_target_pairs={{1,0},{2,1},{3,2},{4,3},{5,4},{6,5},{7,6},{0,7},{9,8},{10,9},{11,1... | collective-permute-start | bytes 39944 | tf_op jit(solution)/shard_map/ppermute | solution.py:27
  103.9 6.4 %collective-permute-start.11 = (f32[1,26,1,128]{3,1,2,0:T(8,128)S(1)}, f32[1,26,1,128]{3,1,2,0:T(8,128)S(1)}, u32[]{:S(2)}, u32[]{:S(2)}) collective-permute-start(f32[1,26,1,128]{3,1,2,0:T(8,128)S(1)} %get-tuple-element.73), channel_id=1, source_target_pairs={{0,1},{1,2},{2,3},{3,4},{4,5},{5,6},{6,7},{7,0},{8,9},{9,10},{10,1... | collective-permute-start | bytes 39944 | tf_op jit(solution)/shard_map/ppermute | solution.py:24
  111.1 3.5 %collective-permute-start.12 = (f32[3,2,2,128]{3,1,2,0:T(2,128)S(1)}, f32[3,2,2,128]{3,1,2,0:T(2,128)S(1)}, u32[]{:S(2)}, u32[]{:S(2)}) collective-permute-start(f32[3,2,2,128]{3,1,2,0:T(2,128)S(1)} %get-tuple-element.56), channel_id=1, source_target_pairs={{0,8},{8,16},{16,24},{24,0},{1,9},{9,17},{17,25},{25,1},{2,10},{10... | collective-permute-start | bytes 18440 | tf_op jit(solution)/shard_map/ppermute | solution.py:24
  111.1 3.5 %collective-permute-start.13 = (f32[3,2,2,128]{3,1,2,0:T(2,128)S(1)}, f32[3,2,2,128]{3,1,2,0:T(2,128)S(1)}, u32[]{:S(2)}, u32[]{:S(2)}) collective-permute-start(f32[3,2,2,128]{3,1,2,0:T(2,128)S(1)} %get-tuple-element.57), channel_id=1, source_target_pairs={{8,0},{16,8},{24,16},{0,24},{9,1},{17,9},{25,17},{1,25},{10,2},{18... | collective-permute-start | bytes 18440 | tf_op jit(solution)/shard_map/ppermute | solution.py:27
  114.6 8.4 %collective-permute-start.14 = (f32[3,28,2,128]{3,1,2,0:T(8,128)S(1)}, f32[3,28,2,128]{3,1,2,0:T(8,128)S(1)}, u32[]{:S(2)}, u32[]{:S(2)}) collective-permute-start(f32[3,28,2,128]{3,1,2,0:T(8,128)S(1)} %pad_maximum_fusion.24), channel_id=1, source_target_pairs={{0,1},{1,2},{2,3},{3,4},{4,5},{5,6},{6,7},{7,0},{8,9},{9,10},{10,1... | collective-permute-start | bytes 258056 | tf_op jit(solution)/shard_map/ppermute | solution.py:24
  114.7 8.4 %collective-permute-start.15 = (f32[3,28,2,128]{3,1,2,0:T(8,128)S(1)}, f32[3,28,2,128]{3,1,2,0:T(8,128)S(1)}, u32[]{:S(2)}, u32[]{:S(2)}) collective-permute-start(f32[3,28,2,128]{3,1,2,0:T(8,128)S(1)} %pad_maximum_fusion.24), channel_id=1, source_target_pairs={{1,0},{2,1},{3,2},{4,3},{5,4},{6,5},{7,6},{0,7},{9,8},{10,9},{11,1... | collective-permute-start | bytes 258056 | tf_op jit(solution)/shard_map/ppermute | solution.py:27
  149.0 2.4 %collective-permute-start.16 = (f32[3,1,2,128]{3,1,2,0:T(1,128)S(1)}, f32[3,1,2,128]{3,1,2,0:T(1,128)S(1)}, u32[]{:S(2)}, u32[]{:S(2)}) collective-permute-start(f32[3,1,2,128]{3,1,2,0:T(1,128)S(1)} %get-tuple-element.49), channel_id=1, source_target_pairs={{8,0},{16,8},{24,16},{0,24},{9,1},{17,9},{25,17},{1,25},{10,2},{18... | collective-permute-start | bytes 9224 | tf_op jit(solution)/shard_map/ppermute | solution.py:27
  150.1 3.0 %collective-permute-start.17 = (f32[3,1,2,128]{3,1,2,0:T(1,128)S(1)}, f32[3,1,2,128]{3,1,2,0:T(1,128)S(1)}, u32[]{:S(2)}, u32[]{:S(2)}) collective-permute-start(f32[3,1,2,128]{3,1,2,0:T(1,128)S(1)} %get-tuple-element.48), channel_id=1, source_target_pairs={{0,8},{8,16},{16,24},{24,0},{1,9},{9,17},{17,25},{25,1},{2,10},{10... | collective-permute-start | bytes 9224 | tf_op jit(solution)/shard_map/ppermute | solution.py:24
  153.1 6.0 %collective-permute-start.18 = (f32[3,26,1,128]{3,1,2,0:T(8,128)S(1)}, f32[3,26,1,128]{3,1,2,0:T(8,128)S(1)}, u32[]{:S(2)}, u32[]{:S(2)}) collective-permute-start(f32[3,26,1,128]{3,1,2,0:T(8,128)S(1)} %get-tuple-element.45), channel_id=1, source_target_pairs={{1,0},{2,1},{3,2},{4,3},{5,4},{6,5},{7,6},{0,7},{9,8},{10,9},{11,1... | collective-permute-start | bytes 119816 | tf_op jit(solution)/shard_map/ppermute | solution.py:27
  157.4 6.8 %collective-permute-start.19 = (f32[3,26,1,128]{3,1,2,0:T(8,128)S(1)}, f32[3,26,1,128]{3,1,2,0:T(8,128)S(1)}, u32[]{:S(2)}, u32[]{:S(2)}) collective-permute-start(f32[3,26,1,128]{3,1,2,0:T(8,128)S(1)} %get-tuple-element.44), channel_id=1, source_target_pairs={{0,1},{1,2},{2,3},{3,4},{4,5},{5,6},{6,7},{7,0},{8,9},{9,10},{10,1... | collective-permute-start | bytes 119816 | tf_op jit(solution)/shard_map/ppermute | solution.py:24
  200.2 1.4 collective-permute-start.20
  200.3 3.0 %collective-permute-start.21 = (f32[1,1,2,128]{3,1,2,0:T(1,128)S(1)}, f32[1,1,2,128]{3,1,2,0:T(1,128)S(1)}, u32[]{:S(2)}, u32[]{:S(2)}) collective-permute-start(f32[1,1,2,128]{3,1,2,0:T(1,128)S(1)} %get-tuple-element.79), channel_id=1, source_target_pairs={{0,8},{8,16},{16,24},{24,0},{1,9},{9,17},{17,25},{25,1},{2,10},{10... | collective-permute-start | bytes 3080 | tf_op jit(solution)/shard_map/ppermute | solution.py:24
  203.4 3.8 %collective-permute-start.22 = (f32[1,26,1,128]{3,1,2,0:T(8,128)S(1)}, f32[1,26,1,128]{3,1,2,0:T(8,128)S(1)}, u32[]{:S(2)}, u32[]{:S(2)}) collective-permute-start(f32[1,26,1,128]{3,1,2,0:T(8,128)S(1)} %get-tuple-element.70), channel_id=1, source_target_pairs={{1,0},{2,1},{3,2},{4,3},{5,4},{6,5},{7,6},{0,7},{9,8},{10,9},{11,1... | collective-permute-start | bytes 39944 | tf_op jit(solution)/shard_map/ppermute | solution.py:27
  204.1 6.4 %collective-permute-start.23 = (f32[1,26,1,128]{3,1,2,0:T(8,128)S(1)}, f32[1,26,1,128]{3,1,2,0:T(8,128)S(1)}, u32[]{:S(2)}, u32[]{:S(2)}) collective-permute-start(f32[1,26,1,128]{3,1,2,0:T(8,128)S(1)} %get-tuple-element.71), channel_id=1, source_target_pairs={{0,1},{1,2},{2,3},{3,4},{4,5},{5,6},{6,7},{7,0},{8,9},{9,10},{10,1... | collective-permute-start | bytes 39944 | tf_op jit(solution)/shard_map/ppermute | solution.py:24
  (2 other events, 1.4 us)
Sparse Core Ops, SparseCore 0:
  11.4 31.5 all-reduce.4
  121.9 26.0 all-reduce.6
where the time goes:
time: 219 us; the launch traced here: 218 us
  waiting for transfers between devices  92.4 us (42%)
  starting transfers between devices  40.4 us (18%)
  blocking collectives  39.7 us (18%)
  between operations  14.9 us (7%)
  other arithmetic  14.5 us (7%)
  local copies, waits for them, and re-layouts  11 us (5%)
  matrix products  5.29 us (2%)
    psum x2, waiting for transfers between devices, from_root(): return lax.psum(block, axis)  39.6 us
    ppermute x12, waiting for transfers between devices, extended_2(): lax.ppermute(lax.slice_in_dim(block, block.shape[dim] - width, None, axis...  27.7 us
    all_to_all x3, blocking collectives, tile_turn(): lax.all_to_all(blocks, 'tile', split_axis=0, concat_axis=0, tiled=True)  27 us
    ppermute x12, starting transfers between devices, extended_2(): lax.ppermute(lax.slice_in_dim(block, 0, width, axis=dim), axis, backward)  23.8 us
    all_to_all x2, blocking collectives, sec_turn(): lax.all_to_all(blocks, 'sec', split_axis=0, concat_axis=0, tiled=True)  12.7 us
    ppermute x12, waiting for transfers between devices, extended_2(): lax.ppermute(lax.slice_in_dim(block, 0, width, axis=dim), axis, backward)  10.9 us
    all_to_all x2, waiting for transfers between devices, sec_turn(): lax.all_to_all(blocks, 'sec', split_axis=0, concat_axis=0, tiled=True)  7.66 us
    ppermute x12, starting transfers between devices, extended_2(): lax.ppermute(lax.slice_in_dim(block, block.shape[dim] - width, None, axis...  6.65 us
  transfers between devices with their start and end apart: 29, of which 24 were waited for; matrix products, arithmetic and copies ran while one was open for 5% of the time, Pallas kernels for 0%

commit v1 on v0

--- a/solution.py
+++ b/solution.py
@@ -1,13 +1,19 @@
+import functools
 import math
 
 import jax
 import jax.numpy as jnp
+import numpy as np
 from jax import lax
+from jax.experimental import pallas as pl
+from jax.experimental.pallas import tpu as pltpu
 from jax.sharding import PartitionSpec as P
 
 STEPS = 2
 KINDS = 16
-
+ROWS = 8
+LANES = 128
+MESH = pl.DeviceIdType.MESH
 
 precise = lax.Precision.HIGHEST
 time_step = 0.1
@@ -201,7 +207,512 @@
     return (current, tendency)
 
 
+def cas_table(first, second, length):
+    angle = 2.0 * np.pi / length * (np.outer(first, second) % length)
+    return np.cos(angle) + np.sin(angle)
+
+
+def halves(table):
+    high = table.astype(np.float32).astype(jnp.bfloat16)
+    low = (table - high.astype(np.float64)).astype(np.float32).astype(jnp.bfloat16)
+    return np.stack([high, low])
+
+
+def tables(sec_count, tile_count, slab_x, tile_y, depth_z):
+    full_x, full_y = slab_x * sec_count, tile_y * tile_count
+    wide_x = -(-full_x // LANES) * LANES
+    planes = tile_y + 2
+    z_at = np.arange(depth_z)
+    cos_z = np.cos(np.pi / depth_z * np.outer(z_at, z_at + 0.5))
+    x_cas = np.zeros((sec_count, LANES, planes * wide_x))
+    for sec in range(sec_count):
+        start = sec * slab_x
+        for plane in range(planes):
+            x_cas[sec, plane * slab_x : (plane + 1) * slab_x, plane * wide_x : plane * wide_x + full_x] = (
+                cas_table(start + np.arange(slab_x), np.arange(full_x), full_x)
+            )
+        for row in range(tile_y):
+            for side, x_at in ((0, start - 1), (1, start + slab_x)):
+                x_cas[
+                    sec,
+                    planes * slab_x + side * tile_y + row,
+                    (row + 1) * wide_x : (row + 1) * wide_x + full_x,
+                ] = cas_table(np.array([x_at % full_x]), np.arange(full_x), full_x)[0]
+    y_blocks = []
+    for plane in range(planes):
+        y_at = (np.arange(tile_count) * tile_y + plane - 1) % full_y
+        y_blocks.append(np.kron(cas_table(np.arange(full_y), y_at, full_y), np.eye(ROWS)))
+    y_cas = np.concatenate(y_blocks, axis=1)
+    k_x, k_y = np.arange(full_x), np.arange(full_y)
+    sin_x = np.where(k_x % (full_x // 2) == 0, 0.0, np.sin(2.0 * np.pi * k_x / full_x) ** 2)
+    sin_y = np.where(k_y % (full_y // 2) == 0, 0.0, np.sin(2.0 * np.pi * k_y / full_y) ** 2)
+    sin_xy = np.ones((full_y * ROWS, wide_x), np.float32)
+    sin_xy[:, :full_x] = np.repeat(sin_y, ROWS)[:, None] + sin_x[None, :]
+    sin_z = np.sin(np.pi * z_at / depth_z) ** 2
+    weight_z = -np.where(z_at == 0, 1.0, 2.0) / (depth_z * full_x * full_y)
+    mode_z = np.stack([sin_z, weight_z]).astype(np.float32)
+    mode_z = np.ascontiguousarray(np.broadcast_to(mode_z[:, :, None], (2, depth_z, wide_x)))
+    lam = fringe_rate * np.sin(np.pi * (np.arange(slab_x) + 0.5) / slab_x) ** 2
+    lam = np.ascontiguousarray(np.broadcast_to(lam.astype(np.float32)[:, None], (slab_x, depth_z)))
+    return halves(cos_z), halves(x_cas), halves(y_cas), halves(y_cas.T), sin_xy, mode_z, lam
+
+
+def split(value):
+    high = value.astype(jnp.bfloat16)
+    return high, (value - high.astype(jnp.float32)).astype(jnp.bfloat16)
+
+
+def dot3(first, second, dims):
+    def dot(one, two):
+        return lax.dot_general(one, two, (dims, ((), ())), preferred_element_type=jnp.float32)
+
+    return dot(first[0], second[0]) + (dot(first[0], second[1]) + dot(first[1], second[0]))
+
+
+NN = ((1,), (0,))
+NT = ((1,), (1,))
+
+
+def slope_z(value, z_sign):
+    depth = value.shape[1]
+    lane = lax.broadcasted_iota(jnp.int32, value.shape, 1)
+    edge = value * z_sign
+    above = jnp.where(lane == depth - 1, edge, pltpu.roll(value, depth - 1, 1))
+    below = jnp.where(lane == 0, edge, pltpu.roll(value, 1, 1))
+    return 0.5 * (above - below)
+
+
+def slope_x(value, low=None, high=None):
+    count = value.shape[0]
+    after = pltpu.roll(value, count - 1, 0)
+    before = pltpu.roll(value, 1, 0)
+    if low is not None:
+        row = lax.broadcasted_iota(jnp.int32, value.shape, 0)
+        after = jnp.where(row == count - 1, high, after)
+        before = jnp.where(row == 0, low, before)
+    return 0.5 * (after - before)
+
+
+def step_kernel(
+    sec_count,
+    tile_count,
+    slab_x,
+    tile_y,
+    depth_z,
+    vel_ref,
+    old_ref,
+    cells_ref,
+    kinds_ref,
+    weights_ref,
+    cos_ref,
+    x_ref,
+    y_ref,
+    yt_ref,
+    sin_xy_ref,
+    mode_z_ref,
+    lam_ref,
+    vel_out,
+    tend_out,
+    wide,
+    target,
+    share,
+    coeffs,
+    plane_in,
+    plane_out,
+    returned,
+    press,
+    thrust,
+    recip,
+    halo_send,
+    halo_recv,
+    target_send,
+    target_recv,
+    mode_send,
+    mode_recv,
+    back_send,
+    back_recv,
+):
+    sec = lax.axis_index("sec")
+    tile = lax.axis_index("tile")
+    devices = sec_count * tile_count
+    me = tile * sec_count + sec
+    owners = depth_z // ROWS
+    spacing = devices // owners
+    planes = tile_y + 2
+    deep = tile_y + 4
+    wide_x = sin_xy_ref.shape[1]
+    group = tile_count * ROWS
+    root = sec_count // 2 - 1
+    fringes = sorted({0, sec_count // 2, 3 * sec_count // 4, sec_count - 1} - {root})
+    is_owner = lax.rem(me, spacing) == 0
+    owner_at = lax.div(me, spacing)
+    in_fringe = functools.reduce(jnp.logical_or, [sec == which for which in fringes])
+    low_sec, high_sec = lax.rem(sec + sec_count - 1, sec_count), lax.rem(sec + 1, sec_count)
+    low_tile, high_tile = lax.rem(tile + tile_count - 1, tile_count), lax.rem(tile + 1, tile_count)
+    end_x = ROWS + slab_x
+    own_x, own_y = slice(ROWS, end_x), slice(2, 2 + tile_y)
+
+    barrier = pltpu.get_barrier_semaphore()
+
+    def greet(ahead, carry):
+        other = lax.rem(me + ahead, devices)
+        pl.semaphore_signal(
+            barrier,
+            inc=1,
+            device_id=(lax.rem(other, sec_count), lax.div(other, sec_count)),
+            device_id_type=MESH,
+        )
+        return carry
+
+    lax.fori_loop(1, devices, greet, 0)
+
+    for part in range(3):
+        for row in range(tile_y):
+            wide[0, part, 2 + row, own_x, :] = vel_ref[part, pl.ds(row, slab_x, stride=tile_y), :]
+    share[...] = jnp.zeros_like(share)
+
+    pl.semaphore_wait(barrier, devices - 1)
+
+    def start_halo(step):
+        xs = {
+            -1: (low_sec, slice(ROWS, 2 * ROWS), slice(end_x, end_x + ROWS)),
+            0: (sec, own_x, own_x),
+            1: (high_sec, slice(end_x - ROWS, end_x), slice(0, ROWS)),
+        }
+        ys = {
+            -1: (low_tile, slice(2, 4), slice(2 + tile_y, deep)),
+            0: (tile, own_y, own_y),
+            1: (high_tile, slice(tile_y, 2 + tile_y), slice(0, 2)),
+        }
+        copies = []
+        for x_way in (-1, 0, 1):
+            for y_way in (-1, 0, 1):
+                if x_way == 0 and y_way == 0:
+                    continue
+                slot = len(copies)
+                to_sec, x_from, x_to = xs[x_way]
+                to_tile, y_from, y_to = ys[y_way]
+                copy = pltpu.make_async_remote_copy(
+                    src_ref=wide.at[step, :, y_from, x_from, :],
+                    dst_ref=wide.at[step, :, y_to, x_to, :],
+                    send_sem=halo_send.at[step, slot],
+                    recv_sem=halo_recv.at[step, slot],
+                    device_id=(to_sec, to_tile),
+                    device_id_type=MESH,
+                )
+                copies.append(copy)
+        sends = [
+            pltpu.make_async_remote_copy(
+                src_ref=wide.at[step, :, own_y, own_x, :],
+                dst_ref=target.at[step],
+                send_sem=target_send.at[step, place],
+                recv_sem=target_recv.at[step],
+                device_id=(which, tile),
+                device_id_type=MESH,
+            )
+            for place, which in enumerate(fringes)
+        ]
+
+        @pl.when(sec == root)
+        def _():
+            for send in sends:
+                send.start()
+
+        for copy in copies:
+            copy.start()
+        return copies, sends
+
+    halo = start_halo(0)
+    pending = [halo]
+
+    cells = cells_ref[...]
+    kinds = kinds_ref[...]
+    weight = jnp.zeros(cells.shape, jnp.float32)
+    for kind in range(KINDS):
+        weight = jnp.where(kinds == kind, weights_ref[kind], weight)
+    weight = jnp.where(cells < slab_x * tile_y * depth_z, weight, 0.0)
+    column = lax.div(cells, depth_z)
+    row_of = lax.rem(column, tile_y) * slab_x + lax.div(column, tile_y)
+    slots = cells.shape[1]
+    hit_row = lax.broadcasted_iota(jnp.int32, (tile_y * slab_x, slots), 0) == row_of
+    hit_z = lax.broadcasted_iota(jnp.int32, (depth_z, slots), 0) == lax.rem(cells, depth_z)
+    hit_z = hit_z.astype(jnp.float32).astype(jnp.bfloat16)
+    rest = jnp.where(hit_row, weight, 0.0)
+    summed = jnp.zeros((tile_y * slab_x, depth_z), jnp.float32)
+    for _ in range(3):
+        piece, rest_next = rest.astype(jnp.bfloat16), None
+        rest_next = rest - piece.astype(jnp.float32)
+        summed = summed + lax.dot_general(
+            piece, hit_z, (NT, ((), ())), preferred_element_type=jnp.float32
+        )
+        rest = rest_next
+    thrust[...] = summed
+
+    @pl.when(is_owner)
+    def _():
+        rows = pl.ds(pl.multiple_of(owner_at * ROWS, ROWS), ROWS)
+        full_y = tile_y * tile_count
+        sum_sin = sin_xy_ref[...] + jnp.concatenate([mode_z_ref[0, rows, :]] * full_y, axis=0)
+        scale = jnp.concatenate([mode_z_ref[1, rows, :]] * full_y, axis=0)
+        zero_mode = sum_sin == 0.0
+        recip[...] = jnp.where(zero_mode, 0.0, scale / jnp.where(zero_mode, 1.0, sum_sin))
+
+    cos_z = (cos_ref[0], cos_ref[1])
+    old = [
+        [old_ref[part, pl.ds(row, slab_x, stride=tile_y), :] for row in range(tile_y)]
+        for part in range(3)
+    ]
+
+    for step in range(STEPS):
+        copies, sends = halo
+
+        @pl.when(in_fringe)
+        def _(step=step):
+            pltpu.make_async_copy(target.at[step], target.at[step], target_recv.at[step]).wait()
+
+        @pl.when(jnp.logical_not(in_fringe))
+        def _(step=step):
+            target[step] = wide[step, :, own_y, own_x, :]
+
+        for copy in copies:
+            copy.wait_recv()
+
+        centre, stress, advect = {}, {}, {}
+        for plane in range(1, deep - 1):
+            here = [wide[step, part, plane] for part in range(3)]
+            d_x = [slope_x(value) for value in here]
+            d_y = [
+                0.5 * (wide[step, part, plane + 1] - wide[step, part, plane - 1])
+                for part in range(3)
+            ]
+            d_z = [slope_z(value, -1.0) for value in here]
+            s_xx, s_yy, s_zz = d_x[0], d_y[1], d_z[2]
+            s_xy = 0.5 * (d_x[1] + d_y[0])
+            s_xz = 0.5 * (d_x[2] + d_z[0])
+            s_yz = 0.5 * (d_y[2] + d_z[1])
+            squared = s_xx * s_xx + s_yy * s_yy + s_zz * s_zz
+            squared = squared + 2.0 * (s_xy * s_xy + s_xz * s_xz + s_yz * s_yz)
+            double = (2.0 * smag_coef) * jnp.sqrt(2.0 * squared + 0.01)
+            stress[plane] = [double * s for s in (s_xx, s_yy, s_zz, s_xy, s_xz, s_yz)]
+            centre[plane] = here
+            advect[plane] = [
+                here[0] * d_x[part] + here[1] * d_y[part] + here[2] * d_z[part]
+                for part in range(3)
+            ]
+        interim, tendency = [], []
+        for row in range(tile_y):
+            plane = 2 + row
+            xx, yy, zz, xy, xz, yz = stress[plane]
+            before, after = stress[plane - 1], stress[plane + 1]
+            push = [
+                slope_x(xx) + 0.5 * (after[3] - before[3]) + slope_z(xz, 0.0),
+                slope_x(xy) + 0.5 * (after[1] - before[1]) + slope_z(yz, 0.0),
+                slope_x(xz) + 0.5 * (after[5] - before[5]) + slope_z(zz, 0.0),
+            ]
+            lam = lam_ref[...]
+            tend, mid = [], []
+            for part in range(3):
+                here = centre[plane][part][own_x]
+                total = (push[part] - advect[plane][part])[own_x]
+                if part == 0:
+                    force = thrust[row * slab_x : (row + 1) * slab_x, :]
+                    total = total - force * here * jnp.abs(here)
+                total = total + lam * (target[step, part, row] - here)
+                tend.append(total)
+                mid.append(here + time_step * (1.5 * total - 0.5 * old[part][row]))
+                if step == STEPS - 1:
+                    tend_out[part, pl.ds(row, slab_x, stride=tile_y), :] = total
+            tendency.append(tend)
+            interim.append(mid)
+        old = [[tendency[row][part] for row in range(tile_y)] for part in range(3)]
+
+        share[0:slab_x, :] = 0.5 * interim[0][1]
+        share[(planes - 1) * slab_x : planes * slab_x, :] = -0.5 * interim[tile_y - 1][1]
+        for row in range(tile_y):
+            along_x, _, along_z = interim[row]
+            total = slope_x(along_x, 0.0, 0.0) + slope_z(along_z, -1.0)
+            if row + 1 < tile_y:
+                total = total + 0.5 * interim[row + 1][1]
+            if row > 0:
+                total = total - 0.5 * interim[row - 1][1]
+            share[(row + 1) * slab_x : (row + 2) * slab_x, :] = total
+            edge = planes * slab_x + row
+            share[edge : edge + 1, :] = 0.5 * along_x[0:1]
+            share[edge + tile_y : edge + tile_y + 1, :] = -0.5 * along_x[slab_x - 1 : slab_x]
+        coeffs[step] = dot3(cos_z, split(share[...]), NT)
+
+        my_rows = pl.ds(pl.multiple_of(tile * ROWS, ROWS), ROWS)
+
+        def send_modes(ahead, carry, step=step):
+            owner = lax.rem(owner_at + ahead, owners)
+            flat = owner * spacing
+            rows = pl.ds(pl.multiple_of(owner * ROWS, ROWS), ROWS)
+
+            @pl.when(flat == me)
+            def _():
+                pltpu.make_async_copy(
+                    coeffs.at[step, rows, :], plane_in.at[step, sec, my_rows, :], mode_recv.at[step]
+                ).start()
+
+            @pl.when(flat != me)
+            def _():
+                pltpu.make_async_remote_copy(
+                    src_ref=coeffs.at[step, rows, :],
+                    dst_ref=plane_in.at[step, sec, my_rows, :],
+                    send_sem=mode_send.at[step],
+                    recv_sem=mode_recv.at[step],
+                    device_id=(lax.rem(flat, sec_count), lax.div(flat, sec_count)),
+                    device_id_type=MESH,
+                ).start()
+
+            return carry
+
+        lax.fori_loop(0, owners, send_modes, 0)
+
+        @pl.when(is_owner)
+        def _(step=step):
+            pltpu.make_async_copy(
+                plane_in.at[step], plane_in.at[step], mode_recv.at[step]
+            ).wait()
+            along_x = jnp.zeros((group, planes * wide_x), jnp.float32)
+            for part in range(sec_count):
+                along_x = along_x + dot3(
+                    split(plane_in[step, part]), (x_ref[0, part], x_ref[1, part]), NN
+                )
+            stacked = jnp.concatenate(
+                [along_x[:, i * wide_x : (i + 1) * wide_x] for i in range(planes)], axis=0
+            )
+            modes = dot3((y_ref[0], y_ref[1]), split(stacked), NN) * recip[...]
+            back_y = dot3((yt_ref[0], yt_ref[1]), split(modes), NN)
+            flat_y = split(
+                jnp.concatenate([back_y[i * group : (i + 1) * group] for i in range(planes)], axis=1)
+            )
+            for part in range(sec_count):
+                plane_out[step, part] = dot3(flat_y, (x_ref[0, part], x_ref[1, part]), NT)
+            rows = pl.ds(pl.multiple_of(owner_at * ROWS, ROWS), ROWS)
+
+            pltpu.make_async_copy(
+                plane_out.at[step, sec, my_rows, :], returned.at[step, rows, :], back_recv.at[step]
+            ).start()
+
+            def send_back(ahead, carry):
+                other = lax.rem(me + ahead, devices)
+                to_sec, to_tile = lax.rem(other, sec_count), lax.div(other, sec_count)
+                pltpu.make_async_remote_copy(
+                    src_ref=plane_out.at[
+                        step, to_sec, pl.ds(pl.multiple_of(to_tile * ROWS, ROWS), ROWS), :
+                    ],
+                    dst_ref=returned.at[step, rows, :],
+                    send_sem=back_send.at[step],
+                    recv_sem=back_recv.at[step],
+                    device_id=(to_sec, to_tile),
+                    device_id_type=MESH,
+                ).start()
+                return carry
+
+            lax.fori_loop(1, devices, send_back, 0)
+
+        pltpu.make_async_copy(returned.at[step], returned.at[step], back_recv.at[step]).wait()
+        press[...] = dot3(split(returned[step].T), cos_z, NN)
+        for row in range(tile_y):
+            here = press[(row + 1) * slab_x : (row + 2) * slab_x, :]
+            edge = planes * slab_x + row
+            slopes = [
+                slope_x(here, press[edge : edge + 1, :], press[edge + tile_y : edge + tile_y + 1, :]),
+                0.5
+                * (
+                    press[(row + 2) * slab_x : (row + 3) * slab_x, :]
+                    - press[row * slab_x : (row + 1) * slab_x, :]
+                ),
+                slope_z(here, 1.0),
+            ]
+            for part in range(3):
+                value = interim[row][part] - slopes[part]
+                if step == STEPS - 1:
+                    vel_out[part, pl.ds(row, slab_x, stride=tile_y), :] = value
+                else:
+                    wide[step + 1, part, 2 + row, own_x, :] = value
+        if step < STEPS - 1:
+            halo = start_halo(step + 1)
+            pending.append(halo)
+
+    for step, (copies, sends) in enumerate(pending):
+        for copy in copies:
+            copy.wait_send()
+
+        @pl.when(sec == root)
+        def _(sends=sends):
+            for send in sends:
+                send.wait_send()
+
+        @pl.when(is_owner)
+        def _(step=step):
+            most = coeffs.at[step, pl.ds(0, (owners - 1) * ROWS), :]
+            pltpu.make_async_copy(most, most, mode_send.at[step]).wait()
+            some = plane_out.at[step, pl.ds(0, sec_count - 1)]
+            pltpu.make_async_copy(some, some, back_send.at[step]).wait()
+            last = plane_out.at[step, sec_count - 1, pl.ds(0, group - ROWS), :]
+            pltpu.make_async_copy(last, last, back_send.at[step]).wait()
+
+        @pl.when(jnp.logical_not(is_owner))
+        def _(step=step):
+            pltpu.make_async_copy(coeffs.at[step], coeffs.at[step], mode_send.at[step]).wait()
+
+
+def direct(sec_count, tile_count, velocity, prev_tendency, disk_cells, disk_kind, rotor_weights):
+    _, slab_x, tile_y, depth_z = velocity.shape
+    constants = [
+        jnp.asarray(table) for table in tables(sec_count, tile_count, slab_x, tile_y, depth_z)
+    ]
+    wide_x = constants[4].shape[1]
+    full_y = tile_y * tile_count
+    group = tile_count * ROWS
+    flat = (3, slab_x * tile_y, depth_z)
+    vmem = pl.BlockSpec(memory_space=pltpu.VMEM)
+    smem = pl.BlockSpec(memory_space=pltpu.SMEM)
+    dma = pltpu.SemaphoreType.DMA
+    outs = pl.pallas_call(
+        functools.partial(step_kernel, sec_count, tile_count, slab_x, tile_y, depth_z),
+        out_shape=[jax.ShapeDtypeStruct(flat, jnp.float32)] * 2,
+        in_specs=[vmem] * 4 + [smem] + [vmem] * len(constants),
+        out_specs=[vmem] * 2,
+        scratch_shapes=[
+            pltpu.VMEM((STEPS, 3, tile_y + 4, slab_x + 2 * ROWS, depth_z), jnp.float32),
+            pltpu.VMEM((STEPS, 3, tile_y, slab_x, depth_z), jnp.float32),
+            pltpu.VMEM((LANES, depth_z), jnp.float32),
+            pltpu.VMEM((STEPS, depth_z, LANES), jnp.float32),
+            pltpu.VMEM((STEPS, sec_count, group, LANES), jnp.float32),
+            pltpu.VMEM((STEPS, sec_count, group, LANES), jnp.float32),
+            pltpu.VMEM((STEPS, depth_z, LANES), jnp.float32),
+            pltpu.VMEM((LANES, depth_z), jnp.float32),
+            pltpu.VMEM((tile_y * slab_x, depth_z), jnp.float32),
+            pltpu.VMEM((full_y * ROWS, wide_x), jnp.float32),
+            dma((STEPS, 8)),
+            dma((STEPS, 8)),
+            dma((STEPS, 4)),
+            dma((STEPS,)),
+            dma((STEPS,)),
+            dma((STEPS,)),
+            dma((STEPS,)),
+            dma((STEPS,)),
+        ],
+        compiler_params=pltpu.CompilerParams(
+            collective_id=0, has_side_effects=True, vmem_limit_bytes=32 * 1024 * 1024
+        ),
+        name="les_steps",
+    )(
+        velocity.reshape(flat),
+        prev_tendency.reshape(flat),
+        disk_cells.reshape(1, -1),
+        disk_kind.reshape(1, -1),
+        rotor_weights,
+        *constants,
+    )
+    return tuple(out.reshape(velocity.shape) for out in outs)
+
+
 def solution(mesh):
+    sec_count, tile_count = mesh.shape["sec"], mesh.shape["tile"]
     in_specs = (
         P(None, "sec", "tile", None),
         P(None, "sec", "tile", None),
@@ -210,4 +721,23 @@
         P(),
     )
     out_specs = (P(None, "sec", "tile", None), P(None, "sec", "tile", None))
-    return jax.shard_map(local, mesh=mesh, in_specs=in_specs, out_specs=out_specs, check_vma=False)
+
+    def pick(velocity, *others):
+        _, slab_x, tile_y, depth_z = velocity.shape
+        owners = depth_z // ROWS
+        fits = (
+            owners <= sec_count * tile_count
+            and (sec_count * tile_count) % owners == 0
+            and depth_z % LANES == 0
+            and slab_x % ROWS == 0
+            and tile_y >= 2
+            and (tile_y + 2) * slab_x + 2 * tile_y <= LANES
+            and tile_y * tile_count * ROWS <= 512
+            and sec_count >= 3
+            and tile_count >= 3
+        )
+        if fits:
+            return direct(sec_count, tile_count, velocity, *others)
+        return local(velocity, *others)
+
+    return jax.shard_map(pick, mesh=mesh, in_specs=in_specs, out_specs=out_specs, check_vma=False)

time: 219 us -> 56 us (0.26)
  waiting for transfers between devices: 92.4 us -> 0 us
  Pallas kernels: 0 us -> 45.5 us
  starting transfers between devices: 40.4 us -> 0 us
  blocking collectives: 39.7 us -> 0 us
  other arithmetic: 14.5 us -> 0 us
  between operations: 14.9 us -> 0.69 us
  matrix products: 5.29 us -> 0 us
    pallas_call x0 -> x1, Pallas kernels: none -> 45.5 us  [direct(): pl.pallas_call(functools.partial(step_kernel, sec_count, tile_count, slab...]
    all_to_all x5 -> x0, blocking collectives: 39.7 us -> none  [the longest x3 27 us: tile_turn(): lax.all_to_all(blocks, 'tile', split_axis=0, concat_axis=0, tiled=True)]
    psum x2 -> x0, waiting for transfers between devices: 39.6 us -> none  [from_root(): return lax.psum(block, axis)]
    ppermute x24 -> x0, waiting for transfers between devices: 38.6 us -> none  [the longest x12 27.7 us: extended_2(): lax.ppermute(lax.slice_in_dim(block, block.shape[dim] - width, None, axis...]
    ppermute x24 -> x0, starting transfers between devices: 30.5 us -> none  [the longest x12 23.8 us: extended_2(): lax.ppermute(lax.slice_in_dim(block, 0, width, axis=dim), axis, backward)]
    all_to_all x3 -> x0, waiting for transfers between devices: 14.2 us -> none  [the longest x2 7.66 us: sec_turn(): lax.all_to_all(blocks, 'sec', split_axis=0, concat_axis=0, tiled=True)]
    all_to_all x3 -> x0, starting transfers between devices: 9.86 us -> none  [the longest x2 6.52 us: sec_turn(): lax.all_to_all(blocks, 'sec', split_axis=0, concat_axis=0, tiled=True)]
    scatter-add x2 -> x0, other arithmetic: 4.7 us -> none  [local(): turbine = jnp.zeros((cell_count,), jnp.float32).at[safe].add(push).reshap...]
  transfers between devices with their start and end apart: 29 -> 0, of which waited for: 24 -> 0; matrix products, arithmetic and copies ran while one was open for 5% -> 0% of each run, Pallas kernels for 0% -> 0%
where the time goes in v1:
time: 56 us; the launch traced here: 55.5 us
  Pallas kernels  45.5 us (81%)
  local copies, waits for them, and re-layouts  9.33 us (17%)
  between operations  0.69 us (1%)
    pallas_call x1, Pallas kernels, direct(): pl.pallas_call(functools.partial(step_kernel, sec_count, tile_count, slab...  45.5 us
    unnamed x26, local copies, waits for them, and re-layouts  9.33 us

profile of v1, /device:TPU:0, one launch (start us, length us, event | category | flops | bytes accessed | tf_op | source)
XLA Modules:
  0.0 55.5 jit_solution(7906478715011753304)
XLA Ops:
  0.6 0.0 copy-start.8
  0.6 0.0 copy-start.10
  0.7 0.0 copy-start.9
  0.7 0.0 copy-start.11
  0.7 0.7 %copy-done.8 = f32[24,128]{1,0:T(8,128)S(1)} copy-done((f32[24,128]{1,0:T(8,128)S(1)}, f32[24,128]{1,0:T(8,128)}, u32[]{:S(2)}) %copy-start.8) | copy-done | bytes 12312
  1.3 0.0 copy-done.10
  1.3 0.0 copy-done.9
  1.3 0.0 copy-done.11
  1.3 0.0 copy-start
  1.4 1.2 %copy-done = bf16[2,4,128,512]{3,2,1,0:T(8,128)(2,1)S(1)} copy-done((bf16[2,4,128,512]{3,2,1,0:T(8,128)(2,1)S(1)}, bf16[2,4,128,512]{3,2,1,0:T(8,128)(2,1)}, u32[]{:S(2)}) %copy-start) | copy-done | bytes 1048600
  2.6 0.0 copy-start.1
  2.6 0.9 %copy-done.1 = f32[2,128,128]{2,1,0:T(8,128)S(1)} copy-done((f32[2,128,128]{2,1,0:T(8,128)S(1)}, f32[2,128,128]{2,1,0:T(8,128)}, u32[]{:S(2)}) %copy-start.1) | copy-done | bytes 131096
  3.5 0.0 copy-start.2
  3.5 0.9 %copy-done.2 = bf16[2,256,128]{2,1,0:T(8,128)(2,1)S(1)} copy-done((bf16[2,256,128]{2,1,0:T(8,128)(2,1)S(1)}, bf16[2,256,128]{2,1,0:T(8,128)(2,1)}, u32[]{:S(2)}) %copy-start.2) | copy-done | bytes 131096
  4.4 0.0 copy-start.3
  4.4 0.9 %copy-done.3 = bf16[2,128,256]{2,1,0:T(8,128)(2,1)S(1)} copy-done((bf16[2,128,256]{2,1,0:T(8,128)(2,1)S(1)}, bf16[2,128,256]{2,1,0:T(8,128)(2,1)}, u32[]{:S(2)}) %copy-start.3) | copy-done | bytes 131096
  5.3 0.0 copy-start.4
  5.3 0.9 %copy-done.4 = f32[3,24,2,128]{3,2,1,0:T(2,128)S(1)} copy-done((f32[3,24,2,128]{3,2,1,0:T(2,128)S(1)}, f32[3,24,2,128]{3,2,1,0:T(2,128)}, u32[]{:S(2)}) %copy-start.4) | copy-done | bytes 73752
  6.2 0.0 copy-start.5
  6.2 0.9 %copy-done.5 = f32[3,24,2,128]{3,2,1,0:T(2,128)S(1)} copy-done((f32[3,24,2,128]{3,2,1,0:T(2,128)S(1)}, f32[3,24,2,128]{3,2,1,0:T(2,128)}, u32[]{:S(2)}) %copy-start.5) | copy-done | bytes 73752
  7.1 0.0 copy-start.6
  7.1 0.8 %copy-done.6 = f32[128,128]{1,0:T(8,128)S(1)} copy-done((f32[128,128]{1,0:T(8,128)S(1)}, f32[128,128]{1,0:T(8,128)}, u32[]{:S(2)}) %copy-start.6) | copy-done | bytes 65560
  7.9 0.0 copy-start.7
  7.9 0.8 %copy-done.7 = bf16[2,128,128]{2,1,0:T(8,128)(2,1)S(1)} copy-done((bf16[2,128,128]{2,1,0:T(8,128)(2,1)S(1)}, bf16[2,128,128]{2,1,0:T(8,128)(2,1)}, u32[]{:S(2)}) %copy-start.7) | copy-done | bytes 65560
  8.7 45.5 %les_steps.1 = (f32[3,48,128]{2,1,0:T(8,128)S(1)}, f32[3,48,128]{2,1,0:T(8,128)S(1)}) custom-call(f32[3,48,128]{2,1,0:T(8,128)S(1)} %bitcast.6, f32[3,48,128]{2,1,0:T(8,128)S(1)} %bitcast.7, s32[1,256]{1,0:T(1,128)S(1)} %bitcast.10, s32[1,256]{1,0:T(1,128)S(1)} %bitcast.11, f32[16]{0:T(128)S(1)} %copy-done.11, bf16[2,128,128]{2,1,0:T(8,128)(2,1)S(1)} %copy-done.7, ...), custom_call_target="tpu_custom_call" | custom-call | tf_op jit(solution)/shard_map/les_steps/pallas_call | solution.py:674
  54.2 0.6 %copy.16 = f32[3,24,2,128]{3,2,1,0:T(2,128)} copy(f32[3,24,2,128]{3,2,1,0:T(2,128)S(1)} %bitcast.9) | data formatting | bytes 147456
  54.9 0.6 %copy.17 = f32[3,24,2,128]{3,2,1,0:T(2,128)} copy(f32[3,24,2,128]{3,2,1,0:T(2,128)S(1)} %bitcast.8) | data formatting | bytes 147456
Async XLA Ops:
  0.6 0.7 %copy-start.8 = (f32[24,128]{1,0:T(8,128)S(1)}, f32[24,128]{1,0:T(8,128)}, u32[]{:S(2)}) copy-start(f32[24,128]{1,0:T(8,128)} %constant.20.clone.lam_ref) | copy-start | bytes 36868
  0.6 0.7 %copy-start.10 = (s32[1,1,256]{2,1,0:T(1,128)S(1)}, s32[1,1,256]{2,1,0:T(1,128)}, u32[]{:S(2)}) copy-start(s32[1,1,256]{2,1,0:T(1,128)} %param.15) | copy-start | bytes 3076
  0.7 0.7 %copy-start.9 = (s32[1,1,256]{2,1,0:T(1,128)S(1)}, s32[1,1,256]{2,1,0:T(1,128)}, u32[]{:S(2)}) copy-start(s32[1,1,256]{2,1,0:T(1,128)} %param.14) | copy-start | bytes 3076
  0.7 0.7 %copy-start.11 = (f32[16]{0:T(128)S(1)}, f32[16]{0:T(128)}, u32[]{:S(2)}) copy-start(f32[16]{0:T(128)} %weights_ref.1) | copy-start | bytes 196
  1.3 1.2 %copy-start = (bf16[2,4,128,512]{3,2,1,0:T(8,128)(2,1)S(1)}, bf16[2,4,128,512]{3,2,1,0:T(8,128)(2,1)}, u32[]{:S(2)}) copy-start(bf16[2,4,128,512]{3,2,1,0:T(8,128)(2,1)} %constant.15.clone.x_ref) | copy-start | bytes 3145732
  2.6 0.9 %copy-start.1 = (f32[2,128,128]{2,1,0:T(8,128)S(1)}, f32[2,128,128]{2,1,0:T(8,128)}, u32[]{:S(2)}) copy-start(f32[2,128,128]{2,1,0:T(8,128)} %constant.19.clone.mode_z_ref) | copy-start | bytes 393220
  3.5 0.9 %copy-start.2 = (bf16[2,256,128]{2,1,0:T(8,128)(2,1)S(1)}, bf16[2,256,128]{2,1,0:T(8,128)(2,1)}, u32[]{:S(2)}) copy-start(bf16[2,256,128]{2,1,0:T(8,128)(2,1)} %constant.17.clone.yt_ref) | copy-start | bytes 393220
  4.4 0.9 %copy-start.3 = (bf16[2,128,256]{2,1,0:T(8,128)(2,1)S(1)}, bf16[2,128,256]{2,1,0:T(8,128)(2,1)}, u32[]{:S(2)}) copy-start(bf16[2,128,256]{2,1,0:T(8,128)(2,1)} %constant.16.clone.y_ref) | copy-start | bytes 393220
  5.3 0.9 %copy-start.4 = (f32[3,24,2,128]{3,2,1,0:T(2,128)S(1)}, f32[3,24,2,128]{3,2,1,0:T(2,128)}, u32[]{:S(2)}) copy-start(f32[3,24,2,128]{3,2,1,0:T(2,128)} %param.12) | copy-start | bytes 221188
  6.2 0.9 %copy-start.5 = (f32[3,24,2,128]{3,2,1,0:T(2,128)S(1)}, f32[3,24,2,128]{3,2,1,0:T(2,128)}, u32[]{:S(2)}) copy-start(f32[3,24,2,128]{3,2,1,0:T(2,128)} %param.13) | copy-start | bytes 221188
  7.1 0.8 %copy-start.6 = (f32[128,128]{1,0:T(8,128)S(1)}, f32[128,128]{1,0:T(8,128)}, u32[]{:S(2)}) copy-start(f32[128,128]{1,0:T(8,128)} %constant.18.clone.sin_xy_ref) | copy-start | bytes 196612
  7.9 0.8 %copy-start.7 = (bf16[2,128,128]{2,1,0:T(8,128)(2,1)S(1)}, bf16[2,128,128]{2,1,0:T(8,128)(2,1)}, u32[]{:S(2)}) copy-start(bf16[2,128,128]{2,1,0:T(8,128)(2,1)} %constant.14.clone.cos_ref) | copy-start | bytes 196612

commit v2 on v1

--- a/solution.py
+++ b/solution.py
@@ -215,29 +215,31 @@
 def halves(table):
     high = table.astype(np.float32).astype(jnp.bfloat16)
     low = (table - high.astype(np.float64)).astype(np.float32).astype(jnp.bfloat16)
-    return np.stack([high, low])
+    stacked = np.concatenate([high, low], axis=0)
+    return np.concatenate(np.split(stacked, stacked.shape[1] // LANES, axis=1), axis=0)
+
+
+def whole(table, columns):
+    count = table.shape[0] * LANES // columns
+    parts = [table[i * count : (i + 1) * count] for i in range(columns // LANES)]
+    return jnp.concatenate(parts, axis=1)
 
 
 def tables(sec_count, tile_count, slab_x, tile_y, depth_z):
     full_x, full_y = slab_x * sec_count, tile_y * tile_count
     wide_x = -(-full_x // LANES) * LANES
-    planes = tile_y + 2
+    planes, block = tile_y + 2, slab_x + ROWS
     z_at = np.arange(depth_z)
     cos_z = np.cos(np.pi / depth_z * np.outer(z_at, z_at + 0.5))
-    x_cas = np.zeros((sec_count, LANES, planes * wide_x))
+    x_cas = np.zeros((sec_count, LANES, wide_x))
     for sec in range(sec_count):
         start = sec * slab_x
+        cells = np.concatenate([start + np.arange(slab_x), [start - 1, start + slab_x]]) % full_x
         for plane in range(planes):
-            x_cas[sec, plane * slab_x : (plane + 1) * slab_x, plane * wide_x : plane * wide_x + full_x] = (
-                cas_table(start + np.arange(slab_x), np.arange(full_x), full_x)
+            x_cas[sec, plane * block : plane * block + slab_x + 2, :full_x] = cas_table(
+                cells, np.arange(full_x), full_x
             )
-        for row in range(tile_y):
-            for side, x_at in ((0, start - 1), (1, start + slab_x)):
-                x_cas[
-                    sec,
-                    planes * slab_x + side * tile_y + row,
-                    (row + 1) * wide_x : (row + 1) * wide_x + full_x,
-                ] = cas_table(np.array([x_at % full_x]), np.arange(full_x), full_x)[0]
+    x_cas = x_cas.reshape(sec_count * LANES, wide_x)
     y_blocks = []
     for plane in range(planes):
         y_at = (np.arange(tile_count) * tile_y + plane - 1) % full_y
@@ -254,7 +256,16 @@
     mode_z = np.ascontiguousarray(np.broadcast_to(mode_z[:, :, None], (2, depth_z, wide_x)))
     lam = fringe_rate * np.sin(np.pi * (np.arange(slab_x) + 0.5) / slab_x) ** 2
     lam = np.ascontiguousarray(np.broadcast_to(lam.astype(np.float32)[:, None], (slab_x, depth_z)))
-    return halves(cos_z), halves(x_cas), halves(y_cas), halves(y_cas.T), sin_xy, mode_z, lam
+    return (
+        halves(cos_z),
+        halves(x_cas),
+        halves(x_cas.T),
+        halves(y_cas),
+        halves(y_cas.T),
+        sin_xy,
+        mode_z,
+        lam,
+    )
 
 
 def split(value):
@@ -262,11 +273,22 @@
     return high, (value - high.astype(jnp.float32)).astype(jnp.bfloat16)
 
 
-def dot3(first, second, dims):
-    def dot(one, two):
-        return lax.dot_general(one, two, (dims, ((), ())), preferred_element_type=jnp.float32)
-
-    return dot(first[0], second[0]) + (dot(first[0], second[1]) + dot(first[1], second[0]))
+def dot(first, second, dims):
+    return lax.dot_general(first, second, (dims, ((), ())), preferred_element_type=jnp.float32)
+
+
+def table_first(table, second, dims):
+    count = table.shape[0] // 2
+    high, low = split(second)
+    both = dot(table, high, dims)
+    return both[:count] + (both[count:] + dot(table[:count], low, dims))
+
+
+def table_second(first, table):
+    count, depth = first.shape[0], table.shape[0] // 2
+    high, low = split(first)
+    both = dot(jnp.concatenate([high, low], axis=0), table[:depth], NN)
+    return both[:count] + (both[count:] + dot(high, table[depth:], NN))
 
 
 NN = ((1,), (0,))
@@ -299,18 +321,19 @@
     slab_x,
     tile_y,
     depth_z,
-    vel_ref,
-    old_ref,
-    cells_ref,
-    kinds_ref,
+    vel_hbm,
+    old_hbm,
+    cells_hbm,
+    kinds_hbm,
     weights_ref,
-    cos_ref,
-    x_ref,
-    y_ref,
-    yt_ref,
-    sin_xy_ref,
-    mode_z_ref,
-    lam_ref,
+    cos_hbm,
+    x_hbm,
+    xt_hbm,
+    y_hbm,
+    yt_hbm,
+    sin_xy_hbm,
+    mode_z_hbm,
+    lam_hbm,
     vel_out,
     tend_out,
     wide,
@@ -323,6 +346,19 @@
     press,
     thrust,
     recip,
+    vel_ref,
+    old_ref,
+    cells_ref,
+    kinds_ref,
+    cos_ref,
+    x_ref,
+    xt_ref,
+    y_ref,
+    yt_ref,
+    sin_xy_ref,
+    mode_z_ref,
+    lam_ref,
+    load_sem,
     halo_send,
     halo_recv,
     target_send,
@@ -340,8 +376,8 @@
     spacing = devices // owners
     planes = tile_y + 2
     deep = tile_y + 4
-    wide_x = sin_xy_ref.shape[1]
     group = tile_count * ROWS
+    block = slab_x + ROWS
     root = sec_count // 2 - 1
     fringes = sorted({0, sec_count // 2, 3 * sec_count // 4, sec_count - 1} - {root})
     is_owner = lax.rem(me, spacing) == 0
@@ -352,6 +388,28 @@
     end_x = ROWS + slab_x
     own_x, own_y = slice(ROWS, end_x), slice(2, 2 + tile_y)
 
+    loads = [
+        pltpu.make_async_copy(source, held, load_sem.at[place])
+        for place, (source, held) in enumerate(
+            (
+                (vel_hbm, vel_ref),
+                (cells_hbm, cells_ref),
+                (kinds_hbm, kinds_ref),
+                (sin_xy_hbm, sin_xy_ref),
+                (mode_z_hbm, mode_z_ref),
+                (old_hbm, old_ref),
+                (lam_hbm, lam_ref),
+                (cos_hbm, cos_ref),
+                (y_hbm, y_ref),
+                (x_hbm, x_ref),
+                (xt_hbm, xt_ref),
+                (yt_hbm, yt_ref),
+            )
+        )
+    ]
+    for load in loads:
+        load.start()
+
     barrier = pltpu.get_barrier_semaphore()
 
     def greet(ahead, carry):
@@ -366,10 +424,11 @@
 
     lax.fori_loop(1, devices, greet, 0)
 
+    share[...] = jnp.zeros_like(share)
+    loads[0].wait()
     for part in range(3):
         for row in range(tile_y):
             wide[0, part, 2 + row, own_x, :] = vel_ref[part, pl.ds(row, slab_x, stride=tile_y), :]
-    share[...] = jnp.zeros_like(share)
 
     pl.semaphore_wait(barrier, devices - 1)
 
@@ -392,6 +451,10 @@
                 slot = len(copies)
                 to_sec, x_from, x_to = xs[x_way]
                 to_tile, y_from, y_to = ys[y_way]
+                if x_way != 0 and y_way == -1:
+                    y_from, y_to = slice(2, 3), slice(2 + tile_y, 3 + tile_y)
+                if x_way != 0 and y_way == 1:
+                    y_from, y_to = slice(1 + tile_y, 2 + tile_y), slice(1, 2)
                 copy = pltpu.make_async_remote_copy(
                     src_ref=wide.at[step, :, y_from, x_from, :],
                     dst_ref=wide.at[step, :, y_to, x_to, :],
@@ -425,6 +488,8 @@
     halo = start_halo(0)
     pending = [halo]
 
+    for load in loads[1:5]:
+        load.wait()
     cells = cells_ref[...]
     kinds = kinds_ref[...]
     weight = jnp.zeros(cells.shape, jnp.float32)
@@ -457,7 +522,8 @@
         zero_mode = sum_sin == 0.0
         recip[...] = jnp.where(zero_mode, 0.0, scale / jnp.where(zero_mode, 1.0, sum_sin))
 
-    cos_z = (cos_ref[0], cos_ref[1])
+    for load in loads[5:]:
+        load.wait()
     old = [
         [old_ref[part, pl.ds(row, slab_x, stride=tile_y), :] for row in range(tile_y)]
         for part in range(3)
@@ -465,14 +531,6 @@
 
     for step in range(STEPS):
         copies, sends = halo
-
-        @pl.when(in_fringe)
-        def _(step=step):
-            pltpu.make_async_copy(target.at[step], target.at[step], target_recv.at[step]).wait()
-
-        @pl.when(jnp.logical_not(in_fringe))
-        def _(step=step):
-            target[step] = wide[step, :, own_y, own_x, :]
 
         for copy in copies:
             copy.wait_recv()
@@ -499,6 +557,15 @@
                 here[0] * d_x[part] + here[1] * d_y[part] + here[2] * d_z[part]
                 for part in range(3)
             ]
+
+        @pl.when(in_fringe)
+        def _(step=step):
+            pltpu.make_async_copy(target.at[step], target.at[step], target_recv.at[step]).wait()
+
+        @pl.when(jnp.logical_not(in_fringe))
+        def _(step=step):
+            target[step] = wide[step, :, own_y, own_x, :]
+
         interim, tendency = [], []
         for row in range(tile_y):
             plane = 2 + row
@@ -527,7 +594,8 @@
         old = [[tendency[row][part] for row in range(tile_y)] for part in range(3)]
 
         share[0:slab_x, :] = 0.5 * interim[0][1]
-        share[(planes - 1) * slab_x : planes * slab_x, :] = -0.5 * interim[tile_y - 1][1]
+        last = (planes - 1) * block
+        share[last : last + slab_x, :] = -0.5 * interim[tile_y - 1][1]
         for row in range(tile_y):
             along_x, _, along_z = interim[row]
             total = slope_x(along_x, 0.0, 0.0) + slope_z(along_z, -1.0)
@@ -535,11 +603,12 @@
                 total = total + 0.5 * interim[row + 1][1]
             if row > 0:
                 total = total - 0.5 * interim[row - 1][1]
-            share[(row + 1) * slab_x : (row + 2) * slab_x, :] = total
-            edge = planes * slab_x + row
+            start = (row + 1) * block
+            edge = start + slab_x
+            share[start:edge, :] = total
             share[edge : edge + 1, :] = 0.5 * along_x[0:1]
-            share[edge + tile_y : edge + tile_y + 1, :] = -0.5 * along_x[slab_x - 1 : slab_x]
-        coeffs[step] = dot3(cos_z, split(share[...]), NT)
+            share[edge + 1 : edge + 2, :] = -0.5 * along_x[slab_x - 1 : slab_x]
+        coeffs[step] = table_first(cos_ref[...], share[...], NT)
 
         my_rows = pl.ds(pl.multiple_of(tile * ROWS, ROWS), ROWS)
 
@@ -574,21 +643,26 @@
             pltpu.make_async_copy(
                 plane_in.at[step], plane_in.at[step], mode_recv.at[step]
             ).wait()
-            along_x = jnp.zeros((group, planes * wide_x), jnp.float32)
+            lane_plane = lax.broadcasted_iota(jnp.int32, (group, LANES), 1) // block
+            arrived = [plane_in[step, part] for part in range(sec_count)]
+            masked = jnp.concatenate(
+                [
+                    jnp.concatenate(
+                        [jnp.where(lane_plane == plane, piece, 0.0) for piece in arrived], axis=1
+                    )
+                    for plane in range(planes)
+                ],
+                axis=0,
+            )
+            modes = table_second(table_first(whole(y_ref[...], planes * group), masked, NN), whole(x_ref[...], recip.shape[1])) * recip[...]
+            spread = table_first(whole(yt_ref[...], recip.shape[0]), table_second(modes, whole(xt_ref[...], sec_count * LANES)), NN)
             for part in range(sec_count):
-                along_x = along_x + dot3(
-                    split(plane_in[step, part]), (x_ref[0, part], x_ref[1, part]), NN
-                )
-            stacked = jnp.concatenate(
-                [along_x[:, i * wide_x : (i + 1) * wide_x] for i in range(planes)], axis=0
-            )
-            modes = dot3((y_ref[0], y_ref[1]), split(stacked), NN) * recip[...]
-            back_y = dot3((yt_ref[0], yt_ref[1]), split(modes), NN)
-            flat_y = split(
-                jnp.concatenate([back_y[i * group : (i + 1) * group] for i in range(planes)], axis=1)
-            )
-            for part in range(sec_count):
-                plane_out[step, part] = dot3(flat_y, (x_ref[0, part], x_ref[1, part]), NT)
+                lanes = slice(part * LANES, (part + 1) * LANES)
+                piece = spread[:group, lanes]
+                for plane in range(1, planes):
+                    other = spread[plane * group : (plane + 1) * group, lanes]
+                    piece = jnp.where(lane_plane == plane, other, piece)
+                plane_out[step, part] = piece
             rows = pl.ds(pl.multiple_of(owner_at * ROWS, ROWS), ROWS)
 
             pltpu.make_async_copy(
@@ -613,17 +687,16 @@
             lax.fori_loop(1, devices, send_back, 0)
 
         pltpu.make_async_copy(returned.at[step], returned.at[step], back_recv.at[step]).wait()
-        press[...] = dot3(split(returned[step].T), cos_z, NN)
+        press[...] = table_second(returned[step].T, cos_ref[...])
         for row in range(tile_y):
-            here = press[(row + 1) * slab_x : (row + 2) * slab_x, :]
-            edge = planes * slab_x + row
+            start = (row + 1) * block
+            edge = start + slab_x
+            here = press[start:edge, :]
+            above = press[start + block : edge + block, :]
+            below = press[start - block : edge - block, :]
             slopes = [
-                slope_x(here, press[edge : edge + 1, :], press[edge + tile_y : edge + tile_y + 1, :]),
-                0.5
-                * (
-                    press[(row + 2) * slab_x : (row + 3) * slab_x, :]
-                    - press[row * slab_x : (row + 1) * slab_x, :]
-                ),
+                slope_x(here, press[edge : edge + 1, :], press[edge + 1 : edge + 2, :]),
+                0.5 * (above - below),
                 slope_z(here, 1.0),
             ]
             for part in range(3):
@@ -664,17 +737,25 @@
     constants = [
         jnp.asarray(table) for table in tables(sec_count, tile_count, slab_x, tile_y, depth_z)
     ]
-    wide_x = constants[4].shape[1]
+    wide_x = constants[5].shape[1]
     full_y = tile_y * tile_count
     group = tile_count * ROWS
     flat = (3, slab_x * tile_y, depth_z)
     vmem = pl.BlockSpec(memory_space=pltpu.VMEM)
+    hbm = pl.BlockSpec(memory_space=pltpu.HBM)
+    operands = [
+        velocity.reshape(flat),
+        prev_tendency.reshape(flat),
+        disk_cells.reshape(1, -1),
+        disk_kind.reshape(1, -1),
+        *constants,
+    ]
     smem = pl.BlockSpec(memory_space=pltpu.SMEM)
     dma = pltpu.SemaphoreType.DMA
     outs = pl.pallas_call(
         functools.partial(step_kernel, sec_count, tile_count, slab_x, tile_y, depth_z),
         out_shape=[jax.ShapeDtypeStruct(flat, jnp.float32)] * 2,
-        in_specs=[vmem] * 4 + [smem] + [vmem] * len(constants),
+        in_specs=[hbm] * 4 + [smem] + [hbm] * len(constants),
         out_specs=[vmem] * 2,
         scratch_shapes=[
             pltpu.VMEM((STEPS, 3, tile_y + 4, slab_x + 2 * ROWS, depth_z), jnp.float32),
@@ -687,6 +768,8 @@
             pltpu.VMEM((LANES, depth_z), jnp.float32),
             pltpu.VMEM((tile_y * slab_x, depth_z), jnp.float32),
             pltpu.VMEM((full_y * ROWS, wide_x), jnp.float32),
+            *[pltpu.VMEM(operand.shape, operand.dtype) for operand in operands],
+            dma((len(operands),)),
             dma((STEPS, 8)),
             dma((STEPS, 8)),
             dma((STEPS, 4)),
@@ -697,17 +780,10 @@
             dma((STEPS,)),
         ],
         compiler_params=pltpu.CompilerParams(
-            collective_id=0, has_side_effects=True, vmem_limit_bytes=32 * 1024 * 1024
+            collective_id=0, has_side_effects=True, vmem_limit_bytes=63 * 1024 * 1024
         ),
         name="les_steps",
-    )(
-        velocity.reshape(flat),
-        prev_tendency.reshape(flat),
-        disk_cells.reshape(1, -1),
-        disk_kind.reshape(1, -1),
-        rotor_weights,
-        *constants,
-    )
+    )(*operands[:4], rotor_weights, *operands[4:])
     return tuple(out.reshape(velocity.shape) for out in outs)
 
 
@@ -731,7 +807,7 @@
             and depth_z % LANES == 0
             and slab_x % ROWS == 0
             and tile_y >= 2
-            and (tile_y + 2) * slab_x + 2 * tile_y <= LANES
+            and (tile_y + 2) * (slab_x + ROWS) <= LANES
             and tile_y * tile_count * ROWS <= 512
             and sec_count >= 3
             and tile_count >= 3

time: 56 us -> 46.9 us (0.84)
  local copies, waits for them, and re-layouts: 9.33 us -> 2.19 us
  Pallas kernels: 45.5 us -> 43.9 us
    unnamed x26 -> x4, local copies, waits for them, and re-layouts: 9.33 us -> 2.19 us
    pallas_call x1, Pallas kernels: 45.5 us -> 43.9 us  [direct(): pl.pallas_call(functools.partial(step_kernel, sec_count, tile_count, slab...]
where the time goes in v2:
time: 46.9 us; the launch traced here: 46.7 us
  Pallas kernels  43.9 us (94%)
  local copies, waits for them, and re-layouts  2.19 us (5%)
  between operations  0.65 us (1%)
    pallas_call x1, Pallas kernels, direct(): pl.pallas_call(functools.partial(step_kernel, sec_count, tile_count, slab...  43.9 us
    unnamed x4, local copies, waits for them, and re-layouts  2.19 us

profile of v2, /device:TPU:0, one launch (start us, length us, event | category | flops | bytes accessed | tf_op | source)
XLA Modules:
  0.0 46.7 jit_solution(1364598097473470078)
XLA Ops:
  0.6 43.9 %les_steps.1 = (f32[3,48,128]{2,1,0:T(8,128)}, f32[3,48,128]{2,1,0:T(8,128)}) custom-call(f32[3,48,128]{2,1,0:T(8,128)} %bitcast.6, f32[3,48,128]{2,1,0:T(8,128)} %bitcast.7, s32[1,256]{1,0:T(1,128)} %bitcast.10, s32[1,256]{1,0:T(1,128)} %bitcast.11, f32[16]{0:T(128)} %weights_ref.1, bf16[256,128]{1,0:T(8,128)(2,1)} %constant.16.clone.cos_hbm, ...), custom_call_target="tpu_custom_call" | custom-call | tf_op jit(solution)/shard_map/les_steps/pallas_call | solution.py:755
  44.5 0.0 copy-start
  44.5 1.6 %copy.17 = f32[3,24,2,128]{3,2,1,0:T(2,128)} copy(f32[3,24,2,128]{3,2,1,0:T(2,128)} %bitcast.9) | data formatting | bytes 147456
  46.1 0.0 copy-done
  46.1 0.6 %copy.18 = f32[3,24,2,128]{3,2,1,0:T(2,128)} copy(f32[3,24,2,128]{3,2,1,0:T(2,128)S(1)} %bitcast.8) | data formatting | bytes 147456
Async XLA Ops:
  44.5 1.6 %copy-start = (f32[3,48,128]{2,1,0:T(8,128)S(1)}, f32[3,48,128]{2,1,0:T(8,128)}, u32[]{:S(2)}) copy-start(f32[3,48,128]{2,1,0:T(8,128)} %get-tuple-element.5) | copy-start | bytes 221188

commit v3 on v2

--- a/solution.py
+++ b/solution.py
@@ -231,15 +231,13 @@
     planes, block = tile_y + 2, slab_x + ROWS
     z_at = np.arange(depth_z)
     cos_z = np.cos(np.pi / depth_z * np.outer(z_at, z_at + 0.5))
-    x_cas = np.zeros((sec_count, LANES, wide_x))
+    x_cas = np.zeros((LANES, wide_x))
     for sec in range(sec_count):
         start = sec * slab_x
         cells = np.concatenate([start + np.arange(slab_x), [start - 1, start + slab_x]]) % full_x
-        for plane in range(planes):
-            x_cas[sec, plane * block : plane * block + slab_x + 2, :full_x] = cas_table(
-                cells, np.arange(full_x), full_x
-            )
-    x_cas = x_cas.reshape(sec_count * LANES, wide_x)
+        x_cas[sec * block : sec * block + slab_x + 2, :full_x] = cas_table(
+            cells, np.arange(full_x), full_x
+        )
     y_blocks = []
     for plane in range(planes):
         y_at = (np.arange(tile_count) * tile_y + plane - 1) % full_y
@@ -334,8 +332,8 @@
     sin_xy_hbm,
     mode_z_hbm,
     lam_hbm,
-    vel_out,
-    tend_out,
+    vel_result,
+    tend_result,
     wide,
     target,
     share,
@@ -358,7 +356,10 @@
     sin_xy_ref,
     mode_z_ref,
     lam_ref,
+    vel_out,
+    tend_out,
     load_sem,
+    result_sem,
     halo_send,
     halo_recv,
     target_send,
@@ -373,15 +374,15 @@
     devices = sec_count * tile_count
     me = tile * sec_count + sec
     owners = depth_z // ROWS
-    spacing = devices // owners
     planes = tile_y + 2
     deep = tile_y + 4
     group = tile_count * ROWS
     block = slab_x + ROWS
     root = sec_count // 2 - 1
     fringes = sorted({0, sec_count // 2, 3 * sec_count // 4, sec_count - 1} - {root})
-    is_owner = lax.rem(me, spacing) == 0
-    owner_at = lax.div(me, spacing)
+    first_tile = (tile_count - owners // sec_count) // 2
+    is_owner = (tile >= first_tile) & (tile < first_tile + owners // sec_count)
+    owner_at = (tile - first_tile) * sec_count + sec
     in_fringe = functools.reduce(jnp.logical_or, [sec == which for which in fringes])
     low_sec, high_sec = lax.rem(sec + sec_count - 1, sec_count), lax.rem(sec + 1, sec_count)
     low_tile, high_tile = lax.rem(tile + tile_count - 1, tile_count), lax.rem(tile + 1, tile_count)
@@ -409,6 +410,11 @@
     ]
     for load in loads:
         load.start()
+
+    results = [
+        pltpu.make_async_copy(vel_out, vel_result, result_sem.at[0]),
+        pltpu.make_async_copy(tend_out, tend_result, result_sem.at[1]),
+    ]
 
     barrier = pltpu.get_barrier_semaphore()
 
@@ -591,6 +597,8 @@
                     tend_out[part, pl.ds(row, slab_x, stride=tile_y), :] = total
             tendency.append(tend)
             interim.append(mid)
+        if step == STEPS - 1:
+            results[1].start()
         old = [[tendency[row][part] for row in range(tile_y)] for part in range(3)]
 
         share[0:slab_x, :] = 0.5 * interim[0][1]
@@ -613,8 +621,8 @@
         my_rows = pl.ds(pl.multiple_of(tile * ROWS, ROWS), ROWS)
 
         def send_modes(ahead, carry, step=step):
-            owner = lax.rem(owner_at + ahead, owners)
-            flat = owner * spacing
+            owner = lax.rem(me + ahead, owners)
+            flat = owner + first_tile * sec_count
             rows = pl.ds(pl.multiple_of(owner * ROWS, ROWS), ROWS)
 
             @pl.when(flat == me)
@@ -643,25 +651,24 @@
             pltpu.make_async_copy(
                 plane_in.at[step], plane_in.at[step], mode_recv.at[step]
             ).wait()
-            lane_plane = lax.broadcasted_iota(jnp.int32, (group, LANES), 1) // block
+            lane_block = lax.broadcasted_iota(jnp.int32, (group, LANES), 1) // block
             arrived = [plane_in[step, part] for part in range(sec_count)]
-            masked = jnp.concatenate(
-                [
-                    jnp.concatenate(
-                        [jnp.where(lane_plane == plane, piece, 0.0) for piece in arrived], axis=1
-                    )
-                    for plane in range(planes)
-                ],
-                axis=0,
-            )
-            modes = table_second(table_first(whole(y_ref[...], planes * group), masked, NN), whole(x_ref[...], recip.shape[1])) * recip[...]
-            spread = table_first(whole(yt_ref[...], recip.shape[0]), table_second(modes, whole(xt_ref[...], sec_count * LANES)), NN)
+            blocks = []
+            for plane in range(planes):
+                piece = pltpu.roll(arrived[0], -plane * block % LANES, 1)
+                for part in range(1, sec_count):
+                    other = pltpu.roll(arrived[part], (part - plane) * block % LANES, 1)
+                    piece = jnp.where(lane_block == part, other, piece)
+                blocks.append(piece)
+            stacked = jnp.concatenate(blocks, axis=0)
+            modes = table_second(table_first(whole(y_ref[...], planes * group), stacked, NN), whole(x_ref[...], recip.shape[1])) * recip[...]
+            spread = table_first(whole(yt_ref[...], recip.shape[0]), table_second(modes, whole(xt_ref[...], LANES)), NN)
             for part in range(sec_count):
-                lanes = slice(part * LANES, (part + 1) * LANES)
-                piece = spread[:group, lanes]
+                piece = pltpu.roll(spread[:group], -part * block % LANES, 1)
                 for plane in range(1, planes):
-                    other = spread[plane * group : (plane + 1) * group, lanes]
-                    piece = jnp.where(lane_plane == plane, other, piece)
+                    other = spread[plane * group : (plane + 1) * group]
+                    other = pltpu.roll(other, (plane - part) * block % LANES, 1)
+                    piece = jnp.where(lane_block == plane, other, piece)
                 plane_out[step, part] = piece
             rows = pl.ds(pl.multiple_of(owner_at * ROWS, ROWS), ROWS)
 
@@ -709,6 +716,7 @@
             halo = start_halo(step + 1)
             pending.append(halo)
 
+    results[0].start()
     for step, (copies, sends) in enumerate(pending):
         for copy in copies:
             copy.wait_send()
@@ -730,6 +738,20 @@
         @pl.when(jnp.logical_not(is_owner))
         def _(step=step):
             pltpu.make_async_copy(coeffs.at[step], coeffs.at[step], mode_send.at[step]).wait()
+
+    for result in results:
+        result.wait()
+
+
+def hand_over(vel_from, tend_from, vel_to, tend_to, sems):
+    copies = [
+        pltpu.make_async_copy(vel_from, vel_to, sems.at[0]),
+        pltpu.make_async_copy(tend_from, tend_to, sems.at[1]),
+    ]
+    for copy in copies:
+        copy.start()
+    for copy in copies:
+        copy.wait()
 
 
 def direct(sec_count, tile_count, velocity, prev_tendency, disk_cells, disk_kind, rotor_weights):
@@ -741,7 +763,6 @@
     full_y = tile_y * tile_count
     group = tile_count * ROWS
     flat = (3, slab_x * tile_y, depth_z)
-    vmem = pl.BlockSpec(memory_space=pltpu.VMEM)
     hbm = pl.BlockSpec(memory_space=pltpu.HBM)
     operands = [
         velocity.reshape(flat),
@@ -756,7 +777,7 @@
         functools.partial(step_kernel, sec_count, tile_count, slab_x, tile_y, depth_z),
         out_shape=[jax.ShapeDtypeStruct(flat, jnp.float32)] * 2,
         in_specs=[hbm] * 4 + [smem] + [hbm] * len(constants),
-        out_specs=[vmem] * 2,
+        out_specs=[hbm] * 2,
         scratch_shapes=[
             pltpu.VMEM((STEPS, 3, tile_y + 4, slab_x + 2 * ROWS, depth_z), jnp.float32),
             pltpu.VMEM((STEPS, 3, tile_y, slab_x, depth_z), jnp.float32),
@@ -769,7 +790,10 @@
             pltpu.VMEM((tile_y * slab_x, depth_z), jnp.float32),
             pltpu.VMEM((full_y * ROWS, wide_x), jnp.float32),
             *[pltpu.VMEM(operand.shape, operand.dtype) for operand in operands],
+            pltpu.VMEM(flat, jnp.float32),
+            pltpu.VMEM(flat, jnp.float32),
             dma((len(operands),)),
+            dma((2,)),
             dma((STEPS, 8)),
             dma((STEPS, 8)),
             dma((STEPS, 4)),
@@ -784,6 +808,14 @@
         ),
         name="les_steps",
     )(*operands[:4], rotor_weights, *operands[4:])
+    outs = pl.pallas_call(
+        hand_over,
+        out_shape=[jax.ShapeDtypeStruct(flat, jnp.float32)] * 2,
+        in_specs=[hbm] * 2,
+        out_specs=[hbm] * 2,
+        scratch_shapes=[dma((2,))],
+        name="hand_over",
+    )(*outs)
     return tuple(out.reshape(velocity.shape) for out in outs)
 
 
@@ -803,7 +835,8 @@
         owners = depth_z // ROWS
         fits = (
             owners <= sec_count * tile_count
-            and (sec_count * tile_count) % owners == 0
+            and owners % sec_count == 0
+            and sec_count * (slab_x + ROWS) <= LANES
             and depth_z % LANES == 0
             and slab_x % ROWS == 0
             and tile_y >= 2

time: 46.9 us -> 48.9 us (1.043)
  Pallas kernels: 43.9 us -> 48.1 us
  local copies, waits for them, and re-layouts: 2.19 us -> 0 us
    pallas_call x0 -> x1, Pallas kernels: none -> 5.59 us  [direct(): pl.pallas_call(hand_over, out_shape=[jax.ShapeDtypeStruct(flat, jnp.float...]
    unnamed x4 -> x0, local copies, waits for them, and re-layouts: 2.19 us -> none
    pallas_call x1, Pallas kernels: 43.9 us -> 42.5 us  [direct(): pl.pallas_call(functools.partial(step_kernel, sec_count, tile_count, slab...]
where the time goes in v3:
time: 48.9 us; the launch traced here: 48.7 us
  Pallas kernels  48.1 us (98%)
  between operations  0.64 us (1%)
    pallas_call x1, Pallas kernels, direct(): pl.pallas_call(functools.partial(step_kernel, sec_count, tile_count, slab...  42.5 us
    pallas_call x1, Pallas kernels, direct(): pl.pallas_call(hand_over, out_shape=[jax.ShapeDtypeStruct(flat, jnp.float...  5.59 us

profile of v3, /device:TPU:0, one launch (start us, length us, event | category | flops | bytes accessed | tf_op | source)
XLA Modules:
  0.0 48.7 jit_solution(8703489498160870609)
XLA Ops:
  0.6 42.5 %les_steps.1 = (f32[3,48,128]{2,1,0:T(8,128)}, f32[3,48,128]{2,1,0:T(8,128)}) custom-call(f32[3,48,128]{2,1,0:T(8,128)} %bitcast.6, f32[3,48,128]{2,1,0:T(8,128)} %bitcast.7, s32[1,256]{1,0:T(1,128)} %bitcast.8, s32[1,256]{1,0:T(1,128)} %bitcast.9, f32[16]{0:T(128)} %weights_ref.1, bf16[256,128]{1,0:T(8,128)(2,1)} %constant.16.clone.cos_hbm, ...), custom_call_target="tpu_custom_call" | custom-call | tf_op jit(solution)/shard_map/les_steps/pallas_call | solution.py:776
  43.2 5.6 %hand_over.1 = (f32[3,48,128]{2,1,0:T(8,128)}, f32[3,48,128]{2,1,0:T(8,128)}) custom-call(f32[3,48,128]{2,1,0:T(8,128)} %get-tuple-element.6.vel_from, f32[3,48,128]{2,1,0:T(8,128)} %get-tuple-element.7.tend_from), custom_call_target="tpu_custom_call" | custom-call | tf_op jit(solution)/shard_map/hand_over/pallas_call | solution.py:811

commit v4 on v3

--- a/solution.py
+++ b/solution.py
@@ -13,6 +13,7 @@
 KINDS = 16
 ROWS = 8
 LANES = 128
+EDGE = 3
 MESH = pl.DeviceIdType.MESH
 
 precise = lax.Precision.HIGHEST
@@ -232,17 +233,23 @@
     z_at = np.arange(depth_z)
     cos_z = np.cos(np.pi / depth_z * np.outer(z_at, z_at + 0.5))
     x_cas = np.zeros((LANES, wide_x))
+    x_back = np.zeros((LANES, wide_x))
     for sec in range(sec_count):
         start = sec * slab_x
         cells = np.concatenate([start + np.arange(slab_x), [start - 1, start + slab_x]]) % full_x
         x_cas[sec * block : sec * block + slab_x + 2, :full_x] = cas_table(
             cells, np.arange(full_x), full_x
         )
+        cells = np.arange(start - EDGE, start + slab_x + EDGE) % full_x
+        x_back[sec * block : sec * block + slab_x + 2 * EDGE, :full_x] = cas_table(
+            cells, np.arange(full_x), full_x
+        )
     y_blocks = []
-    for plane in range(planes):
+    for plane in range(1 - EDGE, planes + EDGE - 1):
         y_at = (np.arange(tile_count) * tile_y + plane - 1) % full_y
         y_blocks.append(np.kron(cas_table(np.arange(full_y), y_at, full_y), np.eye(ROWS)))
-    y_cas = np.concatenate(y_blocks, axis=1)
+    y_cas = np.concatenate(y_blocks[EDGE - 1 : EDGE - 1 + planes], axis=1)
+    y_back = np.concatenate(y_blocks, axis=1).T
     k_x, k_y = np.arange(full_x), np.arange(full_y)
     sin_x = np.where(k_x % (full_x // 2) == 0, 0.0, np.sin(2.0 * np.pi * k_x / full_x) ** 2)
     sin_y = np.where(k_y % (full_y // 2) == 0, 0.0, np.sin(2.0 * np.pi * k_y / full_y) ** 2)
@@ -257,9 +264,9 @@
     return (
         halves(cos_z),
         halves(x_cas),
-        halves(x_cas.T),
+        halves(x_back.T),
         halves(y_cas),
-        halves(y_cas.T),
+        halves(y_back),
         sin_xy,
         mode_z,
         lam,
@@ -339,8 +346,10 @@
     share,
     coeffs,
     plane_in,
-    plane_out,
-    returned,
+    wide_out,
+    last_out,
+    wide_returned,
+    last_returned,
     press,
     thrust,
     recip,
@@ -470,6 +479,11 @@
                     device_id_type=MESH,
                 )
                 copies.append(copy)
+        for copy in copies:
+            copy.start()
+        return copies
+
+    def start_target(step):
         sends = [
             pltpu.make_async_remote_copy(
                 src_ref=wide.at[step, :, own_y, own_x, :],
@@ -487,12 +501,10 @@
             for send in sends:
                 send.start()
 
-        for copy in copies:
-            copy.start()
-        return copies, sends
-
-    halo = start_halo(0)
-    pending = [halo]
+        return sends
+
+    halos = {0: start_halo(0)}
+    targets = {0: start_target(0)}
 
     for load in loads[1:5]:
         load.wait()
@@ -536,10 +548,9 @@
     ]
 
     for step in range(STEPS):
-        copies, sends = halo
-
-        for copy in copies:
-            copy.wait_recv()
+        if step == 0:
+            for copy in halos[0]:
+                copy.wait_recv()
 
         centre, stress, advect = {}, {}, {}
         for plane in range(1, deep - 1):
@@ -645,6 +656,16 @@
             return carry
 
         lax.fori_loop(0, owners, send_modes, 0)
+        final = step == STEPS - 1
+        if not final:
+            for part in range(3):
+                for row in range(tile_y):
+                    wide[step + 1, part, 2 + row, own_x, :] = interim[row][part]
+            halos[step + 1] = start_halo(step + 1)
+        reach = 1 if final else EDGE
+        plane_out, returned = (last_out, last_returned) if final else (wide_out, wide_returned)
+        per_tile = LANES // block
+        back_planes = tile_y + 2 * reach
 
         @pl.when(is_owner)
         def _(step=step):
@@ -662,18 +683,29 @@
                 blocks.append(piece)
             stacked = jnp.concatenate(blocks, axis=0)
             modes = table_second(table_first(whole(y_ref[...], planes * group), stacked, NN), whole(x_ref[...], recip.shape[1])) * recip[...]
-            spread = table_first(whole(yt_ref[...], recip.shape[0]), table_second(modes, whole(xt_ref[...], LANES)), NN)
+            skip = (EDGE - reach) * group
+            kept = back_planes * group
+            back_table = yt_ref[...]
+            half = back_table.shape[0] // 2
+            back_table = jnp.concatenate(
+                [back_table[skip : skip + kept], back_table[half + skip : half + skip + kept]], axis=0
+            )
+            back_x = table_second(modes, whole(xt_ref[...], LANES))
+            spread = table_first(back_table, back_x, NN)
             for part in range(sec_count):
-                piece = pltpu.roll(spread[:group], -part * block % LANES, 1)
-                for plane in range(1, planes):
-                    other = spread[plane * group : (plane + 1) * group]
-                    other = pltpu.roll(other, (plane - part) * block % LANES, 1)
-                    piece = jnp.where(lane_block == plane, other, piece)
-                plane_out[step, part] = piece
+                for first in range(0, back_planes, per_tile):
+                    piece = None
+                    for place in range(min(per_tile, back_planes - first)):
+                        start = (first + place) * group
+                        other = spread[start : start + group]
+                        other = pltpu.roll(other, (place - part) * block % LANES, 1)
+                        piece = other if piece is None else jnp.where(lane_block == place, other, piece)
+                    lanes = slice(first // per_tile * LANES, (first // per_tile + 1) * LANES)
+                    plane_out[part, :, lanes] = piece
             rows = pl.ds(pl.multiple_of(owner_at * ROWS, ROWS), ROWS)
 
             pltpu.make_async_copy(
-                plane_out.at[step, sec, my_rows, :], returned.at[step, rows, :], back_recv.at[step]
+                plane_out.at[sec, my_rows, :], returned.at[rows, :], back_recv.at[step]
             ).start()
 
             def send_back(ahead, carry):
@@ -681,9 +713,9 @@
                 to_sec, to_tile = lax.rem(other, sec_count), lax.div(other, sec_count)
                 pltpu.make_async_remote_copy(
                     src_ref=plane_out.at[
-                        step, to_sec, pl.ds(pl.multiple_of(to_tile * ROWS, ROWS), ROWS), :
+                        to_sec, pl.ds(pl.multiple_of(to_tile * ROWS, ROWS), ROWS), :
                     ],
-                    dst_ref=returned.at[step, rows, :],
+                    dst_ref=returned.at[rows, :],
                     send_sem=back_send.at[step],
                     recv_sem=back_recv.at[step],
                     device_id=(to_sec, to_tile),
@@ -693,33 +725,48 @@
 
             lax.fori_loop(1, devices, send_back, 0)
 
-        pltpu.make_async_copy(returned.at[step], returned.at[step], back_recv.at[step]).wait()
-        press[...] = table_second(returned[step].T, cos_ref[...])
-        for row in range(tile_y):
-            start = (row + 1) * block
-            edge = start + slab_x
-            here = press[start:edge, :]
-            above = press[start + block : edge + block, :]
-            below = press[start - block : edge - block, :]
-            slopes = [
-                slope_x(here, press[edge : edge + 1, :], press[edge + 1 : edge + 2, :]),
-                0.5 * (above - below),
-                slope_z(here, 1.0),
-            ]
-            for part in range(3):
-                value = interim[row][part] - slopes[part]
-                if step == STEPS - 1:
-                    vel_out[part, pl.ds(row, slab_x, stride=tile_y), :] = value
-                else:
-                    wide[step + 1, part, 2 + row, own_x, :] = value
-        if step < STEPS - 1:
-            halo = start_halo(step + 1)
-            pending.append(halo)
+        pltpu.make_async_copy(returned, returned, back_recv.at[step]).wait()
+        columns = returned[...]
+        columns = jnp.concatenate(
+            [columns[:, i : i + LANES].T for i in range(0, columns.shape[1], LANES)], axis=0
+        )
+        press[0 : columns.shape[0], :] = table_second(columns, cos_ref[...])
+
+        def press_slopes(start, count):
+            here = press[start : start + count, :]
+            above = press[start + block : start + block + count, :]
+            below = press[start - block : start - block + count, :]
+            return here, 0.5 * (above - below), slope_z(here, 1.0)
+
+        if final:
+            for row in range(tile_y):
+                start = (row + 1) * block + EDGE
+                here, along_y, along_z = press_slopes(start, slab_x)
+                low = press[start - 1 : start, :]
+                high = press[start + slab_x : start + slab_x + 1, :]
+                slopes = [slope_x(here, low, high), along_y, along_z]
+                for part in range(3):
+                    vel_out[part, pl.ds(row, slab_x, stride=tile_y), :] = (
+                        interim[row][part] - slopes[part]
+                    )
+        else:
+            for copy in halos[step + 1]:
+                copy.wait()
+            span = slice(ROWS - EDGE, ROWS - EDGE + block)
+            for plane in range(deep):
+                here, along_y, along_z = press_slopes((plane + 1) * block, block)
+                slopes = [slope_x(here), along_y, along_z]
+                for part in range(3):
+                    wide[step + 1, part, plane, span, :] = (
+                        wide[step + 1, part, plane, span, :] - slopes[part]
+                    )
+            targets[step + 1] = start_target(step + 1)
 
     results[0].start()
-    for step, (copies, sends) in enumerate(pending):
-        for copy in copies:
-            copy.wait_send()
+    for copy in halos[0]:
+        copy.wait_send()
+    for step, sends in targets.items():
+        plane_out = last_out if step == STEPS - 1 else wide_out
 
         @pl.when(sec == root)
         def _(sends=sends):
@@ -727,12 +774,12 @@
                 send.wait_send()
 
         @pl.when(is_owner)
-        def _(step=step):
+        def _(step=step, plane_out=plane_out):
             most = coeffs.at[step, pl.ds(0, (owners - 1) * ROWS), :]
             pltpu.make_async_copy(most, most, mode_send.at[step]).wait()
-            some = plane_out.at[step, pl.ds(0, sec_count - 1)]
+            some = plane_out.at[pl.ds(0, sec_count - 1)]
             pltpu.make_async_copy(some, some, back_send.at[step]).wait()
-            last = plane_out.at[step, sec_count - 1, pl.ds(0, group - ROWS), :]
+            last = plane_out.at[sec_count - 1, pl.ds(0, group - ROWS), :]
             pltpu.make_async_copy(last, last, back_send.at[step]).wait()
 
         @pl.when(jnp.logical_not(is_owner))
@@ -743,15 +790,9 @@
         result.wait()
 
 
-def hand_over(vel_from, tend_from, vel_to, tend_to, sems):
-    copies = [
-        pltpu.make_async_copy(vel_from, vel_to, sems.at[0]),
-        pltpu.make_async_copy(tend_from, tend_to, sems.at[1]),
-    ]
-    for copy in copies:
-        copy.start()
-    for copy in copies:
-        copy.wait()
+def hand_over(vel_from, tend_from, vel_to, tend_to):
+    vel_to[...] = vel_from[...]
+    tend_to[...] = tend_from[...]
 
 
 def direct(sec_count, tile_count, velocity, prev_tendency, disk_cells, disk_kind, rotor_weights):
@@ -762,7 +803,10 @@
     wide_x = constants[5].shape[1]
     full_y = tile_y * tile_count
     group = tile_count * ROWS
+    wide_lanes = (tile_y + 2 * EDGE) * (slab_x + ROWS)
+    wide_lanes = -(-wide_lanes // LANES) * LANES
     flat = (3, slab_x * tile_y, depth_z)
+    vmem = pl.BlockSpec(memory_space=pltpu.VMEM)
     hbm = pl.BlockSpec(memory_space=pltpu.HBM)
     operands = [
         velocity.reshape(flat),
@@ -784,9 +828,11 @@
             pltpu.VMEM((LANES, depth_z), jnp.float32),
             pltpu.VMEM((STEPS, depth_z, LANES), jnp.float32),
             pltpu.VMEM((STEPS, sec_count, group, LANES), jnp.float32),
-            pltpu.VMEM((STEPS, sec_count, group, LANES), jnp.float32),
-            pltpu.VMEM((STEPS, depth_z, LANES), jnp.float32),
-            pltpu.VMEM((LANES, depth_z), jnp.float32),
+            pltpu.VMEM((sec_count, group, wide_lanes), jnp.float32),
+            pltpu.VMEM((sec_count, group, LANES), jnp.float32),
+            pltpu.VMEM((depth_z, wide_lanes), jnp.float32),
+            pltpu.VMEM((depth_z, LANES), jnp.float32),
+            pltpu.VMEM((wide_lanes, depth_z), jnp.float32),
             pltpu.VMEM((tile_y * slab_x, depth_z), jnp.float32),
             pltpu.VMEM((full_y * ROWS, wide_x), jnp.float32),
             *[pltpu.VMEM(operand.shape, operand.dtype) for operand in operands],
@@ -804,16 +850,15 @@
             dma((STEPS,)),
         ],
         compiler_params=pltpu.CompilerParams(
-            collective_id=0, has_side_effects=True, vmem_limit_bytes=63 * 1024 * 1024
+            collective_id=0, has_side_effects=True, vmem_limit_bytes=60 * 1024 * 1024
         ),
         name="les_steps",
     )(*operands[:4], rotor_weights, *operands[4:])
     outs = pl.pallas_call(
         hand_over,
         out_shape=[jax.ShapeDtypeStruct(flat, jnp.float32)] * 2,
-        in_specs=[hbm] * 2,
-        out_specs=[hbm] * 2,
-        scratch_shapes=[dma((2,))],
+        in_specs=[vmem] * 2,
+        out_specs=[vmem] * 2,
         name="hand_over",
     )(*outs)
     return tuple(out.reshape(velocity.shape) for out in outs)
@@ -837,6 +882,7 @@
             owners <= sec_count * tile_count
             and owners % sec_count == 0
             and sec_count * (slab_x + ROWS) <= LANES
+            and LANES % (slab_x + ROWS) == 0
             and depth_z % LANES == 0
             and slab_x % ROWS == 0
             and tile_y >= 2

time: 48.9 us -> 43 us (0.88)
  Pallas kernels: 48.1 us -> 42.2 us
    pallas_call x1, Pallas kernels: 5.59 us -> 1.58 us  [direct(): pl.pallas_call(hand_over, out_shape=[jax.ShapeDtypeStruct(flat, jnp.float...]
    pallas_call x1, Pallas kernels: 42.5 us -> 40.6 us  [direct(): pl.pallas_call(functools.partial(step_kernel, sec_count, tile_count, slab...]
where the time goes in v4:
time: 43 us; the launch traced here: 42.8 us
  Pallas kernels  42.2 us (98%)
  between operations  0.64 us (1%)
    pallas_call x1, Pallas kernels, direct(): pl.pallas_call(functools.partial(step_kernel, sec_count, tile_count, slab...  40.6 us
    pallas_call x1, Pallas kernels, direct(): pl.pallas_call(hand_over, out_shape=[jax.ShapeDtypeStruct(flat, jnp.float...  1.58 us

profile of v4, /device:TPU:0, one launch (start us, length us, event | category | flops | bytes accessed | tf_op | source)
XLA Modules:
  0.0 42.8 jit_solution(2145228048675016954)
XLA Ops:
  0.6 40.6 %les_steps.1 = (f32[3,48,128]{2,1,0:T(8,128)}, f32[3,48,128]{2,1,0:T(8,128)}) custom-call(f32[3,48,128]{2,1,0:T(8,128)} %bitcast.6, f32[3,48,128]{2,1,0:T(8,128)} %bitcast.7, s32[1,256]{1,0:T(1,128)} %bitcast.8, s32[1,256]{1,0:T(1,128)} %bitcast.9, f32[16]{0:T(128)} %weights_ref.1, bf16[256,128]{1,0:T(8,128)(2,1)} %constant.16.clone.cos_hbm, ...), custom_call_target="tpu_custom_call" | custom-call | tf_op jit(solution)/shard_map/les_steps/pallas_call | solution.py:820
  41.3 1.6 %hand_over.1 = (f32[3,48,128]{2,1,0:T(8,128)}, f32[3,48,128]{2,1,0:T(8,128)}) custom-call(f32[3,48,128]{2,1,0:T(8,128)} %get-tuple-element.6.vel_from, f32[3,48,128]{2,1,0:T(8,128)} %get-tuple-element.7.tend_from), custom_call_target="tpu_custom_call" | custom-call | tf_op jit(solution)/shard_map/hand_over/pallas_call | solution.py:857

commit v5 on v4

--- a/solution.py
+++ b/solution.py
@@ -14,6 +14,7 @@
 ROWS = 8
 LANES = 128
 EDGE = 3
+COPIES = 2
 MESH = pl.DeviceIdType.MESH
 
 precise = lax.Precision.HIGHEST
@@ -249,7 +250,11 @@
         y_at = (np.arange(tile_count) * tile_y + plane - 1) % full_y
         y_blocks.append(np.kron(cas_table(np.arange(full_y), y_at, full_y), np.eye(ROWS)))
     y_cas = np.concatenate(y_blocks[EDGE - 1 : EDGE - 1 + planes], axis=1)
-    y_back = np.concatenate(y_blocks, axis=1).T
+    half = tile_count // COPIES * ROWS
+    y_back = [
+        halves(np.concatenate([y[:, i * half : (i + 1) * half] for y in y_blocks], axis=1).T)
+        for i in range(COPIES)
+    ]
     k_x, k_y = np.arange(full_x), np.arange(full_y)
     sin_x = np.where(k_x % (full_x // 2) == 0, 0.0, np.sin(2.0 * np.pi * k_x / full_x) ** 2)
     sin_y = np.where(k_y % (full_y // 2) == 0, 0.0, np.sin(2.0 * np.pi * k_y / full_y) ** 2)
@@ -266,7 +271,7 @@
         halves(x_cas),
         halves(x_back.T),
         halves(y_cas),
-        halves(y_back),
+        np.concatenate(y_back, axis=0),
         sin_xy,
         mode_z,
         lam,
@@ -392,6 +397,10 @@
     first_tile = (tile_count - owners // sec_count) // 2
     is_owner = (tile >= first_tile) & (tile < first_tile + owners // sec_count)
     owner_at = (tile - first_tile) * sec_count + sec
+    groups = owners // COPIES
+    my_group, my_copy = lax.rem(owner_at, groups), lax.div(owner_at, groups)
+    half_tiles = tile_count // COPIES
+    half_group = half_tiles * ROWS
     in_fringe = functools.reduce(jnp.logical_or, [sec == which for which in fringes])
     low_sec, high_sec = lax.rem(sec + sec_count - 1, sec_count), lax.rem(sec + 1, sec_count)
     low_tile, high_tile = lax.rem(tile + tile_count - 1, tile_count), lax.rem(tile + 1, tile_count)
@@ -533,12 +542,14 @@
 
     @pl.when(is_owner)
     def _():
-        rows = pl.ds(pl.multiple_of(owner_at * ROWS, ROWS), ROWS)
         full_y = tile_y * tile_count
-        sum_sin = sin_xy_ref[...] + jnp.concatenate([mode_z_ref[0, rows, :]] * full_y, axis=0)
-        scale = jnp.concatenate([mode_z_ref[1, rows, :]] * full_y, axis=0)
-        zero_mode = sum_sin == 0.0
-        recip[...] = jnp.where(zero_mode, 0.0, scale / jnp.where(zero_mode, 1.0, sum_sin))
+        for batch in range(COPIES):
+            rows = pl.ds(pl.multiple_of((my_group * COPIES + batch) * ROWS, ROWS), ROWS)
+            sum_sin = sin_xy_ref[...] + jnp.concatenate([mode_z_ref[0, rows, :]] * full_y, axis=0)
+            scale = jnp.concatenate([mode_z_ref[1, rows, :]] * full_y, axis=0)
+            zero_mode = sum_sin == 0.0
+            value = jnp.where(zero_mode, 0.0, scale / jnp.where(zero_mode, 1.0, sum_sin))
+            recip[batch * full_y * ROWS : (batch + 1) * full_y * ROWS, :] = value
 
     for load in loads[5:]:
         load.wait()
@@ -627,35 +638,41 @@
             share[start:edge, :] = total
             share[edge : edge + 1, :] = 0.5 * along_x[0:1]
             share[edge + 1 : edge + 2, :] = -0.5 * along_x[slab_x - 1 : slab_x]
-        coeffs[step] = table_first(cos_ref[...], share[...], NT)
+        coeffs[step] = table_first(cos_ref[...], share[...], NT).reshape(owners, ROWS, LANES)
 
         my_rows = pl.ds(pl.multiple_of(tile * ROWS, ROWS), ROWS)
 
-        def send_modes(ahead, carry, step=step):
-            owner = lax.rem(me + ahead, owners)
+        first_owner = jnp.where(is_owner, owner_at, lax.rem(me, owners))
+
+        def modes_to(owner, step=step):
             flat = owner + first_tile * sec_count
-            rows = pl.ds(pl.multiple_of(owner * ROWS, ROWS), ROWS)
-
-            @pl.when(flat == me)
-            def _():
-                pltpu.make_async_copy(
-                    coeffs.at[step, rows, :], plane_in.at[step, sec, my_rows, :], mode_recv.at[step]
-                ).start()
-
-            @pl.when(flat != me)
-            def _():
-                pltpu.make_async_remote_copy(
-                    src_ref=coeffs.at[step, rows, :],
-                    dst_ref=plane_in.at[step, sec, my_rows, :],
-                    send_sem=mode_send.at[step],
-                    recv_sem=mode_recv.at[step],
-                    device_id=(lax.rem(flat, sec_count), lax.div(flat, sec_count)),
-                    device_id_type=MESH,
-                ).start()
-
+            return pltpu.make_async_remote_copy(
+                src_ref=coeffs.at[step, pl.ds(lax.rem(owner, groups) * COPIES, COPIES)],
+                dst_ref=plane_in.at[step, sec, :, my_rows, :],
+                send_sem=mode_send.at[step],
+                recv_sem=mode_recv.at[step],
+                device_id=(lax.rem(flat, sec_count), lax.div(flat, sec_count)),
+                device_id_type=MESH,
+            )
+
+        def send_modes(ahead, carry):
+            modes_to(lax.rem(first_owner + ahead, owners)).start()
             return carry
 
-        lax.fori_loop(0, owners, send_modes, 0)
+        lax.fori_loop(1, owners, send_modes, 0, unroll=True)
+
+        @pl.when(is_owner)
+        def _(step=step):
+            pltpu.make_async_copy(
+                coeffs.at[step, pl.ds(my_group * COPIES, COPIES)],
+                plane_in.at[step, sec, :, my_rows, :],
+                mode_recv.at[step],
+            ).start()
+
+        @pl.when(jnp.logical_not(is_owner))
+        def _(first_owner=first_owner):
+            modes_to(first_owner).start()
+
         final = step == STEPS - 1
         if not final:
             for part in range(3):
@@ -673,49 +690,74 @@
                 plane_in.at[step], plane_in.at[step], mode_recv.at[step]
             ).wait()
             lane_block = lax.broadcasted_iota(jnp.int32, (group, LANES), 1) // block
-            arrived = [plane_in[step, part] for part in range(sec_count)]
-            blocks = []
-            for plane in range(planes):
-                piece = pltpu.roll(arrived[0], -plane * block % LANES, 1)
-                for part in range(1, sec_count):
-                    other = pltpu.roll(arrived[part], (part - plane) * block % LANES, 1)
-                    piece = jnp.where(lane_block == part, other, piece)
-                blocks.append(piece)
-            stacked = jnp.concatenate(blocks, axis=0)
-            modes = table_second(table_first(whole(y_ref[...], planes * group), stacked, NN), whole(x_ref[...], recip.shape[1])) * recip[...]
-            skip = (EDGE - reach) * group
-            kept = back_planes * group
-            back_table = yt_ref[...]
-            half = back_table.shape[0] // 2
+            batches = []
+            for batch in range(COPIES):
+                arrived = [plane_in[step, part, batch] for part in range(sec_count)]
+                blocks = []
+                for plane in range(planes):
+                    piece = pltpu.roll(arrived[0], -plane * block % LANES, 1)
+                    for part in range(1, sec_count):
+                        other = pltpu.roll(arrived[part], (part - plane) * block % LANES, 1)
+                        piece = jnp.where(lane_block == part, other, piece)
+                    blocks.append(piece)
+                batches.append(jnp.concatenate(blocks, axis=0))
+            along_y = table_first(
+                whole(y_ref[...], planes * group), jnp.concatenate(batches, axis=1), NN
+            )
+            along_y = jnp.concatenate(
+                [along_y[:, i * LANES : (i + 1) * LANES] for i in range(COPIES)], axis=0
+            )
+            modes = table_second(along_y, whole(x_ref[...], recip.shape[1])) * recip[...]
+            back_x = table_second(modes, whole(xt_ref[...], LANES))
+            count = back_x.shape[0] // COPIES
+            back_x = jnp.concatenate(
+                [back_x[i * count : (i + 1) * count] for i in range(COPIES)], axis=1
+            )
+            skip = (EDGE - reach) * half_group
+            kept = back_planes * half_group
+            full = (tile_y + 2 * EDGE) * half_group
+            high_at = pl.multiple_of(my_copy * 2 * full + skip, 2 * ROWS)
+            low_at = pl.multiple_of(my_copy * 2 * full + full + skip, 2 * ROWS)
             back_table = jnp.concatenate(
-                [back_table[skip : skip + kept], back_table[half + skip : half + skip + kept]], axis=0
+                [yt_ref[pl.ds(high_at, kept), :], yt_ref[pl.ds(low_at, kept), :]], axis=0
             )
-            back_x = table_second(modes, whole(xt_ref[...], LANES))
             spread = table_first(back_table, back_x, NN)
-            for part in range(sec_count):
-                for first in range(0, back_planes, per_tile):
-                    piece = None
-                    for place in range(min(per_tile, back_planes - first)):
-                        start = (first + place) * group
-                        other = spread[start : start + group]
-                        other = pltpu.roll(other, (place - part) * block % LANES, 1)
-                        piece = other if piece is None else jnp.where(lane_block == place, other, piece)
-                    lanes = slice(first // per_tile * LANES, (first // per_tile + 1) * LANES)
-                    plane_out[part, :, lanes] = piece
-            rows = pl.ds(pl.multiple_of(owner_at * ROWS, ROWS), ROWS)
+            back_block = lane_block[:half_group]
+            for batch in range(COPIES):
+                for part in range(sec_count):
+                    for first in range(0, back_planes, per_tile):
+                        piece = None
+                        for place in range(min(per_tile, back_planes - first)):
+                            start = (first + place) * half_group
+                            other = spread[
+                                start : start + half_group, batch * LANES : (batch + 1) * LANES
+                            ]
+                            other = pltpu.roll(other, (place - part) * block % LANES, 1)
+                            if piece is None:
+                                piece = other
+                            else:
+                                piece = jnp.where(back_block == place, other, piece)
+                        lanes = slice(first // per_tile * LANES, (first // per_tile + 1) * LANES)
+                        plane_out[part, batch, :, lanes] = piece
+            rows = pl.ds(my_group * COPIES, COPIES)
+            half_devices = half_tiles * sec_count
+            my_place = me - my_copy * half_devices
+
+            def out_rows(place):
+                start = lax.div(place, sec_count) * ROWS
+                return pl.ds(pl.multiple_of(start, ROWS), ROWS)
 
             pltpu.make_async_copy(
-                plane_out.at[sec, my_rows, :], returned.at[rows, :], back_recv.at[step]
+                plane_out.at[sec, :, out_rows(my_place), :], returned.at[rows], back_recv.at[step]
             ).start()
 
             def send_back(ahead, carry):
-                other = lax.rem(me + ahead, devices)
-                to_sec, to_tile = lax.rem(other, sec_count), lax.div(other, sec_count)
+                place = lax.rem(my_place + ahead, half_devices)
+                to_sec = lax.rem(place, sec_count)
+                to_tile = lax.div(place, sec_count) + my_copy * half_tiles
                 pltpu.make_async_remote_copy(
-                    src_ref=plane_out.at[
-                        to_sec, pl.ds(pl.multiple_of(to_tile * ROWS, ROWS), ROWS), :
-                    ],
-                    dst_ref=returned.at[rows, :],
+                    src_ref=plane_out.at[to_sec, :, out_rows(place), :],
+                    dst_ref=returned.at[rows],
                     send_sem=back_send.at[step],
                     recv_sem=back_recv.at[step],
                     device_id=(to_sec, to_tile),
@@ -723,10 +765,10 @@
                 ).start()
                 return carry
 
-            lax.fori_loop(1, devices, send_back, 0)
+            lax.fori_loop(1, half_devices, send_back, 0, unroll=True)
 
         pltpu.make_async_copy(returned, returned, back_recv.at[step]).wait()
-        columns = returned[...]
+        columns = returned[...].reshape(depth_z, returned.shape[2])
         columns = jnp.concatenate(
             [columns[:, i : i + LANES].T for i in range(0, columns.shape[1], LANES)], axis=0
         )
@@ -775,16 +817,18 @@
 
         @pl.when(is_owner)
         def _(step=step, plane_out=plane_out):
-            most = coeffs.at[step, pl.ds(0, (owners - 1) * ROWS), :]
+            pltpu.make_async_copy(coeffs.at[step], coeffs.at[step], mode_send.at[step]).wait()
+            most = coeffs.at[step, pl.ds(0, owners - COPIES)]
             pltpu.make_async_copy(most, most, mode_send.at[step]).wait()
             some = plane_out.at[pl.ds(0, sec_count - 1)]
             pltpu.make_async_copy(some, some, back_send.at[step]).wait()
-            last = plane_out.at[sec_count - 1, pl.ds(0, group - ROWS), :]
+            last = plane_out.at[sec_count - 1, :, pl.ds(0, half_group - ROWS), :]
             pltpu.make_async_copy(last, last, back_send.at[step]).wait()
 
         @pl.when(jnp.logical_not(is_owner))
         def _(step=step):
-            pltpu.make_async_copy(coeffs.at[step], coeffs.at[step], mode_send.at[step]).wait()
+            for _ in range(COPIES):
+                pltpu.make_async_copy(coeffs.at[step], coeffs.at[step], mode_send.at[step]).wait()
 
     for result in results:
         result.wait()
@@ -826,15 +870,15 @@
             pltpu.VMEM((STEPS, 3, tile_y + 4, slab_x + 2 * ROWS, depth_z), jnp.float32),
             pltpu.VMEM((STEPS, 3, tile_y, slab_x, depth_z), jnp.float32),
             pltpu.VMEM((LANES, depth_z), jnp.float32),
-            pltpu.VMEM((STEPS, depth_z, LANES), jnp.float32),
-            pltpu.VMEM((STEPS, sec_count, group, LANES), jnp.float32),
-            pltpu.VMEM((sec_count, group, wide_lanes), jnp.float32),
-            pltpu.VMEM((sec_count, group, LANES), jnp.float32),
-            pltpu.VMEM((depth_z, wide_lanes), jnp.float32),
-            pltpu.VMEM((depth_z, LANES), jnp.float32),
+            pltpu.VMEM((STEPS, depth_z // ROWS, ROWS, LANES), jnp.float32),
+            pltpu.VMEM((STEPS, sec_count, COPIES, group, LANES), jnp.float32),
+            pltpu.VMEM((sec_count, COPIES, group // COPIES, wide_lanes), jnp.float32),
+            pltpu.VMEM((sec_count, COPIES, group // COPIES, LANES), jnp.float32),
+            pltpu.VMEM((depth_z // ROWS, ROWS, wide_lanes), jnp.float32),
+            pltpu.VMEM((depth_z // ROWS, ROWS, LANES), jnp.float32),
             pltpu.VMEM((wide_lanes, depth_z), jnp.float32),
             pltpu.VMEM((tile_y * slab_x, depth_z), jnp.float32),
-            pltpu.VMEM((full_y * ROWS, wide_x), jnp.float32),
+            pltpu.VMEM((COPIES * full_y * ROWS, wide_x), jnp.float32),
             *[pltpu.VMEM(operand.shape, operand.dtype) for operand in operands],
             pltpu.VMEM(flat, jnp.float32),
             pltpu.VMEM(flat, jnp.float32),
@@ -880,7 +924,8 @@
         owners = depth_z // ROWS
         fits = (
             owners <= sec_count * tile_count
-            and owners % sec_count == 0
+            and owners % (COPIES * sec_count) == 0
+            and tile_count % (2 * COPIES) == 0
             and sec_count * (slab_x + ROWS) <= LANES
             and LANES % (slab_x + ROWS) == 0
             and depth_z % LANES == 0

time: 43 us -> 44.5 us (1.035)
  Pallas kernels: 42.2 us -> 43.6 us
    pallas_call x1, Pallas kernels: 40.6 us -> 42 us  [direct(): pl.pallas_call(functools.partial(step_kernel, sec_count, tile_count, slab...]
where the time goes in v5:
time: 44.5 us; the launch traced here: 44.3 us
  Pallas kernels  43.6 us (98%)
  between operations  0.64 us (1%)
    pallas_call x1, Pallas kernels, direct(): pl.pallas_call(functools.partial(step_kernel, sec_count, tile_count, slab...  42 us
    pallas_call x1, Pallas kernels, direct(): pl.pallas_call(hand_over, out_shape=[jax.ShapeDtypeStruct(flat, jnp.float...  1.58 us

profile of v5, /device:TPU:0, one launch (start us, length us, event | category | flops | bytes accessed | tf_op | source)
XLA Modules:
  0.0 44.3 jit_solution(4575191982957401041)
XLA Ops:
  0.6 42.0 %les_steps.1 = (f32[3,48,128]{2,1,0:T(8,128)}, f32[3,48,128]{2,1,0:T(8,128)}) custom-call(f32[3,48,128]{2,1,0:T(8,128)} %bitcast.6, f32[3,48,128]{2,1,0:T(8,128)} %bitcast.7, s32[1,256]{1,0:T(1,128)} %bitcast.8, s32[1,256]{1,0:T(1,128)} %bitcast.9, f32[16]{0:T(128)} %weights_ref.1, bf16[256,128]{1,0:T(8,128)(2,1)} %constant.16.clone.cos_hbm, ...), custom_call_target="tpu_custom_call" | custom-call | tf_op jit(solution)/shard_map/les_steps/pallas_call | solution.py:864
  42.7 1.6 %hand_over.1 = (f32[3,48,128]{2,1,0:T(8,128)}, f32[3,48,128]{2,1,0:T(8,128)}) custom-call(f32[3,48,128]{2,1,0:T(8,128)} %get-tuple-element.6.vel_from, f32[3,48,128]{2,1,0:T(8,128)} %get-tuple-element.7.tend_from), custom_call_target="tpu_custom_call" | custom-call | tf_op jit(solution)/shard_map/hand_over/pallas_call | solution.py:901

commit v6 on v4

--- a/solution.py
+++ b/solution.py
@@ -369,6 +369,8 @@
     tend_out,
     load_sem,
     result_sem,
+    corner_out,
+    corner_in,
     halo_send,
     halo_recv,
     target_send,
@@ -440,6 +442,7 @@
     lax.fori_loop(1, devices, greet, 0)
 
     share[...] = jnp.zeros_like(share)
+    corner_out[...] = jnp.zeros_like(corner_out)
     loads[0].wait()
     for part in range(3):
         for row in range(tile_y):
@@ -466,13 +469,20 @@
                 slot = len(copies)
                 to_sec, x_from, x_to = xs[x_way]
                 to_tile, y_from, y_to = ys[y_way]
-                if x_way != 0 and y_way == -1:
-                    y_from, y_to = slice(2, 3), slice(2 + tile_y, 3 + tile_y)
-                if x_way != 0 and y_way == 1:
-                    y_from, y_to = slice(1 + tile_y, 2 + tile_y), slice(1, 2)
+                source = wide.at[step, :, y_from, x_from, :]
+                end = wide.at[step, :, y_to, x_to, :]
+                if x_way != 0 and y_way != 0:
+                    corner = x_way + 1 + (y_way + 1) // 2
+                    plane = 2 if y_way < 0 else 1 + tile_y
+                    row = ROWS if x_way < 0 else end_x - 1
+                    for part in range(3):
+                        corner_out[step, corner, part : part + 1, :] = wide[
+                            step, part, plane, row : row + 1, :
+                        ]
+                    source, end = corner_out.at[step, corner], corner_in.at[step, corner]
                 copy = pltpu.make_async_remote_copy(
-                    src_ref=wide.at[step, :, y_from, x_from, :],
-                    dst_ref=wide.at[step, :, y_to, x_to, :],
+                    src_ref=source,
+                    dst_ref=end,
                     send_sem=halo_send.at[step, slot],
                     recv_sem=halo_recv.at[step, slot],
                     device_id=(to_sec, to_tile),
@@ -482,6 +492,17 @@
         for copy in copies:
             copy.start()
         return copies
+
+    def unpack_corners(step):
+        for x_way in (-1, 1):
+            for y_way in (-1, 1):
+                corner = x_way + 1 + (y_way + 1) // 2
+                plane = 2 + tile_y if y_way < 0 else 1
+                row = end_x if x_way < 0 else ROWS - 1
+                for part in range(3):
+                    wide[step, part, plane, row : row + 1, :] = corner_in[
+                        step, corner, part : part + 1, :
+                    ]
 
     def start_target(step):
         sends = [
@@ -551,6 +572,7 @@
         if step == 0:
             for copy in halos[0]:
                 copy.wait_recv()
+            unpack_corners(0)
 
         centre, stress, advect = {}, {}, {}
         for plane in range(1, deep - 1):
@@ -631,31 +653,36 @@
 
         my_rows = pl.ds(pl.multiple_of(tile * ROWS, ROWS), ROWS)
 
-        def send_modes(ahead, carry, step=step):
-            owner = lax.rem(me + ahead, owners)
+        first_owner = jnp.where(is_owner, owner_at, lax.rem(me, owners))
+
+        def modes_to(owner, step=step):
             flat = owner + first_tile * sec_count
-            rows = pl.ds(pl.multiple_of(owner * ROWS, ROWS), ROWS)
-
-            @pl.when(flat == me)
-            def _():
-                pltpu.make_async_copy(
-                    coeffs.at[step, rows, :], plane_in.at[step, sec, my_rows, :], mode_recv.at[step]
-                ).start()
-
-            @pl.when(flat != me)
-            def _():
-                pltpu.make_async_remote_copy(
-                    src_ref=coeffs.at[step, rows, :],
-                    dst_ref=plane_in.at[step, sec, my_rows, :],
-                    send_sem=mode_send.at[step],
-                    recv_sem=mode_recv.at[step],
-                    device_id=(lax.rem(flat, sec_count), lax.div(flat, sec_count)),
-                    device_id_type=MESH,
-                ).start()
-
+            return pltpu.make_async_remote_copy(
+                src_ref=coeffs.at[step, pl.ds(pl.multiple_of(owner * ROWS, ROWS), ROWS), :],
+                dst_ref=plane_in.at[step, sec, my_rows, :],
+                send_sem=mode_send.at[step],
+                recv_sem=mode_recv.at[step],
+                device_id=(lax.rem(flat, sec_count), lax.div(flat, sec_count)),
+                device_id_type=MESH,
+            )
+
+        def send_modes(ahead, carry):
+            modes_to(lax.rem(first_owner + ahead, owners)).start()
             return carry
 
-        lax.fori_loop(0, owners, send_modes, 0)
+        lax.fori_loop(1, owners, send_modes, 0, unroll=True)
+
+        @pl.when(is_owner)
+        def _(step=step):
+            rows = pl.ds(pl.multiple_of(owner_at * ROWS, ROWS), ROWS)
+            pltpu.make_async_copy(
+                coeffs.at[step, rows, :], plane_in.at[step, sec, my_rows, :], mode_recv.at[step]
+            ).start()
+
+        @pl.when(jnp.logical_not(is_owner))
+        def _(first_owner=first_owner):
+            modes_to(first_owner).start()
+
         final = step == STEPS - 1
         if not final:
             for part in range(3):
@@ -723,7 +750,7 @@
                 ).start()
                 return carry
 
-            lax.fori_loop(1, devices, send_back, 0)
+            lax.fori_loop(1, devices, send_back, 0, unroll=True)
 
         pltpu.make_async_copy(returned, returned, back_recv.at[step]).wait()
         columns = returned[...]
@@ -752,15 +779,17 @@
         else:
             for copy in halos[step + 1]:
                 copy.wait()
+            unpack_corners(step + 1)
             span = slice(ROWS - EDGE, ROWS - EDGE + block)
-            for plane in range(deep):
+            for plane in sorted(range(deep), key=lambda at: not 2 <= at < 2 + tile_y):
+                if plane == 0:
+                    targets[step + 1] = start_target(step + 1)
                 here, along_y, along_z = press_slopes((plane + 1) * block, block)
                 slopes = [slope_x(here), along_y, along_z]
                 for part in range(3):
                     wide[step + 1, part, plane, span, :] = (
                         wide[step + 1, part, plane, span, :] - slopes[part]
                     )
-            targets[step + 1] = start_target(step + 1)
 
     results[0].start()
     for copy in halos[0]:
@@ -790,9 +819,24 @@
         result.wait()
 
 
-def hand_over(vel_from, tend_from, vel_to, tend_to):
-    vel_to[...] = vel_from[...]
-    tend_to[...] = tend_from[...]
+def hand_over(vel_from, tend_from, vel_to, tend_to, held, in_sems, out_sems):
+    pieces = []
+    for place, (source, end) in enumerate(((vel_from, vel_to), (tend_from, tend_to))):
+        for part in range(3):
+            slot = 3 * place + part
+            pieces.append(
+                (
+                    pltpu.make_async_copy(source.at[part], held.at[slot], in_sems.at[slot]),
+                    pltpu.make_async_copy(held.at[slot], end.at[part], out_sems.at[slot]),
+                )
+            )
+    for arrive, _ in pieces:
+        arrive.start()
+    for arrive, leave in pieces:
+        arrive.wait()
+        leave.start()
+    for _, leave in pieces:
+        leave.wait()
 
 
 def direct(sec_count, tile_count, velocity, prev_tendency, disk_cells, disk_kind, rotor_weights):
@@ -806,7 +850,6 @@
     wide_lanes = (tile_y + 2 * EDGE) * (slab_x + ROWS)
     wide_lanes = -(-wide_lanes // LANES) * LANES
     flat = (3, slab_x * tile_y, depth_z)
-    vmem = pl.BlockSpec(memory_space=pltpu.VMEM)
     hbm = pl.BlockSpec(memory_space=pltpu.HBM)
     operands = [
         velocity.reshape(flat),
@@ -840,6 +883,8 @@
             pltpu.VMEM(flat, jnp.float32),
             dma((len(operands),)),
             dma((2,)),
+            pltpu.VMEM((STEPS, 4, ROWS, depth_z), jnp.float32),
+            pltpu.VMEM((STEPS, 4, ROWS, depth_z), jnp.float32),
             dma((STEPS, 8)),
             dma((STEPS, 8)),
             dma((STEPS, 4)),
@@ -857,8 +902,10 @@
     outs = pl.pallas_call(
         hand_over,
         out_shape=[jax.ShapeDtypeStruct(flat, jnp.float32)] * 2,
-        in_specs=[vmem] * 2,
-        out_specs=[vmem] * 2,
+        in_specs=[hbm] * 2,
+        out_specs=[hbm] * 2,
+        scratch_shapes=[pltpu.VMEM((6, *flat[1:]), jnp.float32), dma((6,)), dma((6,))],
+        compiler_params=pltpu.CompilerParams(vmem_limit_bytes=60 * 1024 * 1024),
         name="hand_over",
     )(*outs)
     return tuple(out.reshape(velocity.shape) for out in outs)

time: 43 us -> 41.8 us (0.972)
  Pallas kernels: 42.2 us -> 41 us
    pallas_call x1, Pallas kernels: 40.6 us -> 39.4 us  [direct(): pl.pallas_call(functools.partial(step_kernel, sec_count, tile_count, slab...]
where the time goes in v6:
time: 41.8 us; the launch traced here: 41.6 us
  Pallas kernels  41 us (98%)
  between operations  0.64 us (2%)
    pallas_call x1, Pallas kernels, direct(): pl.pallas_call(functools.partial(step_kernel, sec_count, tile_count, slab...  39.4 us
    pallas_call x1, Pallas kernels, direct(): pl.pallas_call(hand_over, out_shape=[jax.ShapeDtypeStruct(flat, jnp.float...  1.54 us

profile of v6, /device:TPU:0, one launch (start us, length us, event | category | flops | bytes accessed | tf_op | source)
XLA Modules:
  0.0 41.6 jit_solution(6306349706080167179)
XLA Ops:
  0.6 39.4 %les_steps.1 = (f32[3,48,128]{2,1,0:T(8,128)}, f32[3,48,128]{2,1,0:T(8,128)}) custom-call(f32[3,48,128]{2,1,0:T(8,128)} %bitcast.6, f32[3,48,128]{2,1,0:T(8,128)} %bitcast.7, s32[1,256]{1,0:T(1,128)} %bitcast.8, s32[1,256]{1,0:T(1,128)} %bitcast.9, f32[16]{0:T(128)} %weights_ref.1, bf16[256,128]{1,0:T(8,128)(2,1)} %constant.16.clone.cos_hbm, ...), custom_call_target="tpu_custom_call" | custom-call | tf_op jit(solution)/shard_map/les_steps/pallas_call | solution.py:863
  40.1 1.5 %hand_over.1 = (f32[3,48,128]{2,1,0:T(8,128)}, f32[3,48,128]{2,1,0:T(8,128)}) custom-call(f32[3,48,128]{2,1,0:T(8,128)} %get-tuple-element.6.vel_from, f32[3,48,128]{2,1,0:T(8,128)} %get-tuple-element.7.tend_from), custom_call_target="tpu_custom_call" | custom-call | tf_op jit(solution)/shard_map/hand_over/pallas_call | solution.py:902

commit v7 on v6

--- a/solution.py
+++ b/solution.py
@@ -462,7 +462,7 @@
             1: (high_tile, slice(tile_y, 2 + tile_y), slice(0, 2)),
         }
         copies = []
-        for x_way in (-1, 0, 1):
+        for x_way in (0, -1, 1):
             for y_way in (-1, 0, 1):
                 if x_way == 0 and y_way == 0:
                     continue
@@ -653,7 +653,8 @@
 
         my_rows = pl.ds(pl.multiple_of(tile * ROWS, ROWS), ROWS)
 
-        first_owner = jnp.where(is_owner, owner_at, lax.rem(me, owners))
+        far_half = jnp.where(tile < tile_count // 2, 0, owners // 2)
+        first_owner = jnp.where(is_owner, owner_at, lax.rem(me, owners // 2) + far_half)
 
         def modes_to(owner, step=step):
             flat = owner + first_tile * sec_count
@@ -666,11 +667,8 @@
                 device_id_type=MESH,
             )
 
-        def send_modes(ahead, carry):
+        for ahead in (*range(owners // 2, owners), *range(1, owners // 2)):
             modes_to(lax.rem(first_owner + ahead, owners)).start()
-            return carry
-
-        lax.fori_loop(1, owners, send_modes, 0, unroll=True)
 
         @pl.when(is_owner)
         def _(step=step):
@@ -735,8 +733,9 @@
                 plane_out.at[sec, my_rows, :], returned.at[rows, :], back_recv.at[step]
             ).start()
 
-            def send_back(ahead, carry):
-                other = lax.rem(me + ahead, devices)
+            def send_back(count, carry):
+                away = lax.div(count + 1, 2) * (1 - 2 * lax.rem(count, 2))
+                other = lax.rem(me + devices // 2 + away + devices, devices)
                 to_sec, to_tile = lax.rem(other, sec_count), lax.div(other, sec_count)
                 pltpu.make_async_remote_copy(
                     src_ref=plane_out.at[
@@ -750,7 +749,7 @@
                 ).start()
                 return carry
 
-            lax.fori_loop(1, devices, send_back, 0, unroll=True)
+            lax.fori_loop(0, devices - 1, send_back, 0, unroll=True)
 
         pltpu.make_async_copy(returned, returned, back_recv.at[step]).wait()
         columns = returned[...]

time: 41.8 us -> 42.6 us (1.019)
  Pallas kernels: 41 us -> 41.8 us
    pallas_call x1, Pallas kernels: 39.4 us -> 40.3 us  [direct(): pl.pallas_call(functools.partial(step_kernel, sec_count, tile_count, slab...]
where the time goes in v7:
time: 42.6 us; the launch traced here: 42.4 us
  Pallas kernels  41.8 us (98%)
  between operations  0.64 us (2%)
    pallas_call x1, Pallas kernels, direct(): pl.pallas_call(functools.partial(step_kernel, sec_count, tile_count, slab...  40.3 us
    pallas_call x1, Pallas kernels, direct(): pl.pallas_call(hand_over, out_shape=[jax.ShapeDtypeStruct(flat, jnp.float...  1.54 us

profile of v7, /device:TPU:0, one launch (start us, length us, event | category | flops | bytes accessed | tf_op | source)
XLA Modules:
  0.0 42.4 jit_solution(16202302248486166725)
XLA Ops:
  0.6 40.3 %les_steps.1 = (f32[3,48,128]{2,1,0:T(8,128)}, f32[3,48,128]{2,1,0:T(8,128)}) custom-call(f32[3,48,128]{2,1,0:T(8,128)} %bitcast.6, f32[3,48,128]{2,1,0:T(8,128)} %bitcast.7, s32[1,256]{1,0:T(1,128)} %bitcast.8, s32[1,256]{1,0:T(1,128)} %bitcast.9, f32[16]{0:T(128)} %weights_ref.1, bf16[256,128]{1,0:T(8,128)(2,1)} %constant.16.clone.cos_hbm, ...), custom_call_target="tpu_custom_call" | custom-call | tf_op jit(solution)/shard_map/les_steps/pallas_call | solution.py:862
  40.9 1.5 %hand_over.1 = (f32[3,48,128]{2,1,0:T(8,128)}, f32[3,48,128]{2,1,0:T(8,128)}) custom-call(f32[3,48,128]{2,1,0:T(8,128)} %get-tuple-element.6.vel_from, f32[3,48,128]{2,1,0:T(8,128)} %get-tuple-element.7.tend_from), custom_call_target="tpu_custom_call" | custom-call | tf_op jit(solution)/shard_map/hand_over/pallas_call | solution.py:901

commit v8 on v6

--- a/solution.py
+++ b/solution.py
@@ -462,7 +462,7 @@
             1: (high_tile, slice(tile_y, 2 + tile_y), slice(0, 2)),
         }
         copies = []
-        for x_way in (-1, 0, 1):
+        for x_way in (0, -1, 1):
             for y_way in (-1, 0, 1):
                 if x_way == 0 and y_way == 0:
                     continue

time: 41.8 us -> 41.8 us (level)
  no operation moved by 1% of the time
where the time goes in v8:
time: 41.8 us; the launch traced here: 41.6 us
  Pallas kernels  41 us (98%)
  between operations  0.64 us (2%)
    pallas_call x1, Pallas kernels, direct(): pl.pallas_call(functools.partial(step_kernel, sec_count, tile_count, slab...  39.4 us
    pallas_call x1, Pallas kernels, direct(): pl.pallas_call(hand_over, out_shape=[jax.ShapeDtypeStruct(flat, jnp.float...  1.54 us

profile of v8, /device:TPU:0, one launch (start us, length us, event | category | flops | bytes accessed | tf_op | source)
XLA Modules:
  0.0 41.6 jit_solution(18217975681306275020)
XLA Ops:
  0.6 39.4 %les_steps.1 = (f32[3,48,128]{2,1,0:T(8,128)}, f32[3,48,128]{2,1,0:T(8,128)}) custom-call(f32[3,48,128]{2,1,0:T(8,128)} %bitcast.6, f32[3,48,128]{2,1,0:T(8,128)} %bitcast.7, s32[1,256]{1,0:T(1,128)} %bitcast.8, s32[1,256]{1,0:T(1,128)} %bitcast.9, f32[16]{0:T(128)} %weights_ref.1, bf16[256,128]{1,0:T(8,128)(2,1)} %constant.16.clone.cos_hbm, ...), custom_call_target="tpu_custom_call" | custom-call | tf_op jit(solution)/shard_map/les_steps/pallas_call | solution.py:863
  40.1 1.5 %hand_over.1 = (f32[3,48,128]{2,1,0:T(8,128)}, f32[3,48,128]{2,1,0:T(8,128)}) custom-call(f32[3,48,128]{2,1,0:T(8,128)} %get-tuple-element.6.vel_from, f32[3,48,128]{2,1,0:T(8,128)} %get-tuple-element.7.tend_from), custom_call_target="tpu_custom_call" | custom-call | tf_op jit(solution)/shard_map/hand_over/pallas_call | solution.py:902
